TPU v7x, 256 devices: a whole 4x4x8 slice. The times are simulated.
256 devices in a mesh: row: 8 (over z), col: 32 (over y, x, core).
Axes of the slice: x: 4, y: 4, z: 8, core: 2. Of those that a mesh axis runs over, the one named last changes fastest.
Arguments:
- precision_diag: float32 [256, 256, 256], P(('row', 'col')), may hold values from -0.1 to 4.6, as said below
- precision_pairs: float32 [256, 7, 256, 256], P(('row', 'col')), may hold values from -0.024 to 0.024
- pattern_cols: int32 [256, 7], P(('row', 'col')), may hold values from -1 to 255, as said below
- newton_diag: float32 [256, 256, 256], P(('row', 'col')), may hold values from -0.1 to 0.1, as said below
- newton_pairs: float32 [256, 7, 256, 256], P(('row', 'col')), may hold values from -0.006 to 0.006
- warm_start: float32 [256, 96, 256], P(('row', 'col')), may hold values from -15 to 15
- target_rows: int32 [96], replicated, may hold values from 0 to 65535, as said below
Outputs:
- inverse_panel: float32 [256, 96, 256], P(('row', 'col'))
- hessian_block: float32 [96, 96], P('row', 'col')
Inputs may be any that keep to these rules, and one draw needn't show every extreme that they name: `pattern_cols`: each row lists its live entries first and -1 for the rest; it has 4 to 7 live entries, some row exactly 7 and some fewer. The live entries of block row I are distinct, differ from I, and lie in the group of 32 consecutive block rows that holds I (groups start at multiples of 32). `precision_diag`: each tile is symmetric, and X is positive definite. `newton_diag`: each tile is symmetric. `target_rows`: the 96 entries are distinct rows of X.
All inputs are finite; a program needn't handle non-finite values.
Results may differ from a plain program's by a relative error of at most 0.0003.
Values sent between devices are 32-bit elements; how exact they have to be, the bound alone decides.
A program may use at most 64 MiB of HBM per device.

v0:
```python
import jax
import jax.numpy as jnp
from jax import lax
from jax.sharding import PartitionSpec as P

HIGHEST = lax.Precision.HIGHEST


def apply_blocks(blocks, diag_tiles, pair_tiles, local_cols, weights):
    gathered = lax.all_gather(blocks, "col", axis=0, tiled=True)
    picked = jnp.take(gathered, local_cols, axis=0) * weights
    own_rows = jnp.einsum("icb,iab->ica", blocks, diag_tiles, precision=HIGHEST)
    own_rows = own_rows + jnp.einsum("ikcb,ikab->ica", picked, pair_tiles, precision=HIGHEST)
    moved_terms = jnp.einsum("icb,ikba->ikca", blocks, pair_tiles, precision=HIGHEST) * weights
    partial_value = (
        jnp.zeros_like(gathered)
        .at[local_cols.reshape(-1)]
        .add(moved_terms.reshape((-1,) + blocks.shape[1:]))
    )
    return own_rows + lax.psum_scatter(partial_value, "col", scatter_dimension=0, tiled=True)


def column_dots(first, second):
    return jnp.sum(first * second, axis=(0, 2))


def residual_norm(residual):
    return lax.psum(column_dots(residual, residual), ("row", "col"))


def on_device(
    precision_diag,
    precision_pairs,
    pattern_cols,
    newton_diag,
    newton_pairs,
    warm_start,
    target_rows,
):
    rows_dev = warm_start.shape[0]
    block_size = warm_start.shape[2]
    cols_count = lax.axis_size("col")
    first_block = (lax.axis_index("row") * cols_count + lax.axis_index("col")) * rows_dev
    group_first = lax.axis_index("row") * cols_count * rows_dev
    live_mask = pattern_cols >= 0
    local_cols = jnp.where(live_mask, pattern_cols - group_first, 0)
    weights = live_mask.astype(jnp.float32)[:, :, None, None]
    global_rows = (
        first_block * block_size + jnp.arange(rows_dev * block_size, dtype=jnp.int32)
    ).reshape(rows_dev, 1, block_size)
    unit_columns = (global_rows == target_rows[None, :, None]).astype(jnp.float32)

    def precision_apply(blocks):
        return apply_blocks(blocks, precision_diag, precision_pairs, local_cols, weights)

    solution = warm_start
    residual = unit_columns - precision_apply(solution)
    norm_now = residual_norm(residual)
    direction = residual
    for iteration in range(2):
        images = precision_apply(direction)
        curvature = lax.psum(column_dots(direction, images), ("row", "col"))
        step_size = norm_now / curvature
        solution = solution + step_size[None, :, None] * direction
        if iteration == 0:
            residual = residual - step_size[None, :, None] * images
            norm_next = residual_norm(residual)
            direction = residual + (norm_next / norm_now)[None, :, None] * direction
            norm_now = norm_next
    newton_image = apply_blocks(solution, newton_diag, newton_pairs, local_cols, weights)
    hessian_fragment = jnp.einsum("icb,idb->cd", solution, newton_image, precision=HIGHEST)
    spread_cols = lax.psum_scatter(hessian_fragment, "col", scatter_dimension=1, tiled=True)
    hessian = lax.psum_scatter(spread_cols, "row", scatter_dimension=0, tiled=True)
    return (solution, hessian)


def solution(mesh):
    placed = (
        P(("row", "col"), None, None),
        P(("row", "col"), None, None, None),
        P(("row", "col"), None),
        P(("row", "col"), None, None),
        P(("row", "col"), None, None, None),
        P(("row", "col"), None, None),
        P(),
    )
    return jax.shard_map(
        on_device,
        mesh=mesh,
        in_specs=placed,
        out_specs=(P(("row", "col"), None, None), P("row", "col")),
        check_vma=False,
    )
```

profile of v0, /device:TPU:1, one launch (start us, length us, event | category | flops | bytes accessed | tf_op | source)
XLA Modules:
  0.0 947.9 jit_solution(14139409423691666153)
XLA Ops:
  8.7 2.1 fusion.49
  10.8 2.1 broadcast.116.clone
  12.9 2.9 scatter_fusion
  15.9 49.0 %all-gather.5.cloned.1.call-done = f32[32,96,256]{2,1,0:T(8,128)} async-done(((f32[1,96,256]{2,1,0:T(8,128)}), f32[32,96,256]{2,1,0:T(8,128)}) %all-gather.5.cloned.1.call-update) | async-done | bytes 3145744 | tf_op jit(solution)/shard_map/all_gather | solution.py:10
  64.9 2.5 gather_fusion
  69.2 85.0 %reduce-scatter.6.cloned.1.call-done = f32[1,96,256]{2,1,0:T(8,128)} async-done(((f32[32,96,256]{2,1,0:T(8,128)}), f32[1,96,256]{2,1,0:T(8,128)}) %reduce-scatter.6.cloned.1.call-update) | async-done | bytes 98320 | tf_op jit(solution)/shard_map/reduce_scatter | solution.py:20
  154.2 1.9 fusion.69
  156.2 2.0 fusion.43
  158.3 2.1 broadcast.116.clone.1
  160.3 2.9 scatter_fusion.1
  163.3 46.0 %all-gather.7.cloned.1.call-done = f32[32,96,256]{2,1,0:T(8,128)} async-done(((f32[1,96,256]{2,1,0:T(8,128)}), f32[32,96,256]{2,1,0:T(8,128)}) %all-gather.7.cloned.1.call-update) | async-done | bytes 3145744 | tf_op jit(solution)/shard_map/all_gather | solution.py:10
  209.3 2.5 gather_fusion.1
  211.8 1.8 fusion.55
  213.6 85.4 %reduce-scatter.8.cloned.1.call-done = f32[1,96,256]{2,1,0:T(8,128)} async-done(((f32[32,96,256]{2,1,0:T(8,128)}), f32[1,96,256]{2,1,0:T(8,128)}) %reduce-scatter.8.cloned.1.call-update) | async-done | bytes 98320 | tf_op jit(solution)/shard_map/reduce_scatter | solution.py:20
  300.4 77.2 %all-reduce.2 = (f32[96]{0:T(128)S(1)}, f32[96]{0:T(128)S(1)}) all-reduce(f32[96]{0:T(128)S(1)} %get-tuple-element.4, f32[96]{0:T(128)S(1)} %get-tuple-element.3), channel_id=1, replica_groups=mesh['row'=8,'col'=32] {'row','col'}, use_global_device_ids=true, to_apply=%region_3.5 | all-reduce | flops 192 | bytes 1536 | tf_op jit(solution)/shard_map/psum | solution.py:28
  377.7 73.3 %psum.30 = f32[96]{0:T(128)S(1)} all-reduce(f32[96]{0:T(128)S(1)} %multiply_reduce_fusion), channel_id=1, replica_groups=mesh['row'=8,'col'=32] {'row','col'}, use_global_device_ids=true, to_apply=%region_9.11 | all-reduce | flops 96 | bytes 768 | tf_op jit(solution)/shard_map/psum | solution.py:28
  451.8 2.0 fusion.37
  453.8 2.1 broadcast.116.clone.2
  455.9 2.9 scatter_fusion.2
  459.1 39.3 %all-gather.9.cloned.1.call-done = f32[32,96,256]{2,1,0:T(8,128)} async-done(((f32[1,96,256]{2,1,0:T(8,128)}), f32[32,96,256]{2,1,0:T(8,128)}) %all-gather.9.cloned.1.call-update) | async-done | bytes 3145744 | tf_op jit(solution)/shard_map/all_gather | solution.py:10
  498.4 2.5 gather_fusion.2
  502.7 84.9 %reduce-scatter.10.cloned.1.call-done = f32[1,96,256]{2,1,0:T(8,128)} async-done(((f32[32,96,256]{2,1,0:T(8,128)}), f32[1,96,256]{2,1,0:T(8,128)}) %reduce-scatter.10.cloned.1.call-update) | async-done | bytes 98320 | tf_op jit(solution)/shard_map/reduce_scatter | solution.py:20
  589.0 77.2 %psum.31 = f32[96]{0:T(128)S(1)} all-reduce(f32[96]{0:T(128)S(1)} %fusion.75), channel_id=1, replica_groups=mesh['row'=8,'col'=32] {'row','col'}, use_global_device_ids=true, to_apply=%region_13.15 | all-reduce | flops 96 | bytes 768 | tf_op jit(solution)/shard_map/psum | solution.py:62
  667.0 2.7 fusion.31
  669.7 2.1 broadcast.116
  671.8 2.9 scatter_fusion.3
  677.9 36.3 %all-gather.11.cloned.1.call-done = f32[32,96,256]{2,1,0:T(8,128)} async-done(((f32[1,96,256]{2,1,0:T(8,128)}), f32[32,96,256]{2,1,0:T(8,128)}) %all-gather.11.cloned.1.call-update) | async-done | bytes 3145744 | tf_op jit(solution)/shard_map/all_gather | solution.py:10
  714.2 2.5 gather_fusion.3
  716.6 3.3 fusion.61
  720.0 84.0 %reduce-scatter.12.cloned.1.call-done = f32[1,96,256]{2,1,0:T(8,128)} async-done(((f32[32,96,256]{2,1,0:T(8,128)}), f32[1,96,256]{2,1,0:T(8,128)}) %reduce-scatter.12.cloned.1.call-update) | async-done | bytes 98320 | tf_op jit(solution)/shard_map/reduce_scatter | solution.py:20
  805.5 120.9 %all-reduce = f32[96,96]{0,1:T(8,128)S(1)} all-reduce(f32[96,96]{0,1:T(8,128)S(1)} %fusion.105), channel_id=6, replica_groups=mesh['row'=8,'col'=32] {'col'}, use_global_device_ids=true, to_apply=%region_16.18.clone | all-reduce | flops 9216 | bytes 73728
  926.4 14.0 %all-reduce.1 = f32[96,3]{0,1:T(4,128)S(1)} all-reduce(f32[96,3]{0,1:T(4,128)S(1)} %constant_dynamic-slice_fusion.1), channel_id=7, replica_groups=mesh['row'=8,'col'=32] {'row'}, use_global_device_ids=true, to_apply=%region_17.19.clone | all-reduce | flops 288 | bytes 2304
  (57 shorter events, 14.2 us)
Async XLA Ops:
  7.2 1.5 copy-start
  7.2 57.7 %all-gather.5.cloned.1.call-start = ((), (), s32[]{:S(2)}) async-start(), calls=%async_computation.4 | async-start | bytes 3244032 | tf_op jit(solution)/shard_map/all_gather | solution.py:10
  7.9 146.3 %reduce-scatter.6.cloned.1.call-start = ((), (), s32[]{:S(2)}) async-start(), calls=%async_computation.5 | async-start | bytes 3244032 | tf_op jit(solution)/shard_map/reduce_scatter | solution.py:20
  15.8 193.5 %all-gather.7.cloned.1.call-start = ((), (), s32[]{:S(2)}) async-start(), calls=%async_computation.6 | async-start | bytes 3244032 | tf_op jit(solution)/shard_map/all_gather | solution.py:10
  15.9 138.3 %copy-start.4 = (f32[1,256,256]{2,1,0:T(8,128)S(1)}, f32[1,256,256]{2,1,0:T(8,128)}, u32[]{:S(2)}) copy-start(f32[1,256,256]{2,1,0:T(8,128)} %param.9) | copy-start | bytes 786436
  15.9 138.3 %copy-start.5 = (f32[1,96,256]{2,1,0:T(8,128)S(1)}, f32[1,96,256]{2,1,0:T(8,128)}, u32[]{:S(2)}) copy-start(f32[1,96,256]{2,1,0:T(8,128)} %param.14) | copy-start | bytes 294916
  15.9 138.3 %copy-start.7 = (s32[96]{0:T(128)S(1)}, s32[96]{0:T(128)}, u32[]{:S(2)}) copy-start(s32[96]{0:T(128)} %param.15) | copy-start | bytes 1156
  156.2 142.8 %reduce-scatter.8.cloned.1.call-start = ((), (), s32[]{:S(2)}) async-start(), calls=%async_computation.7 | async-start | bytes 3244032 | tf_op jit(solution)/shard_map/reduce_scatter | solution.py:20
  163.2 135.7 %copy-start.1 = (f32[1,96,256]{2,1,0:T(8,128)S(1)}, f32[1,96,256]{2,1,0:T(8,128)}, u32[]{:S(2)}) copy-start(f32[1,96,256]{2,1,0:T(8,128)} %fusion.69) | copy-start | bytes 294916
  163.3 335.2 %all-gather.9.cloned.1.call-start = ((), (), s32[]{:S(2)}) async-start(), calls=%async_computation.8 | async-start | bytes 3244032 | tf_op jit(solution)/shard_map/all_gather | solution.py:10
  451.8 135.8 %reduce-scatter.10.cloned.1.call-start = ((), (), s32[]{:S(2)}) async-start(), calls=%async_computation.9 | async-start | bytes 3244032 | tf_op jit(solution)/shard_map/reduce_scatter | solution.py:20
  458.8 128.8 %copy-start.3 = (f32[1,96,256]{2,1,0:T(8,128)S(1)}, f32[1,96,256]{2,1,0:T(8,128)}, u32[]{:S(2)}) copy-start(f32[1,96,256]{2,1,0:T(8,128)} %multiply_add_fusion.1) | copy-start | bytes 294916
  458.8 255.3 %all-gather.11.cloned.1.call-start = ((), (), s32[]{:S(2)}) async-start(), calls=%async_computation.10 | async-start | bytes 3244032 | tf_op jit(solution)/shard_map/all_gather | solution.py:10
  667.0 137.0 %reduce-scatter.12.cloned.1.call-start = ((), (), s32[]{:S(2)}) async-start(), calls=%async_computation.11 | async-start | bytes 3244032 | tf_op jit(solution)/shard_map/reduce_scatter | solution.py:20
  674.7 0.7 copy-start.9
  674.7 1.3 copy-start.8
  677.9 126.1 %copy-start.2 = (f32[1,96,256]{2,1,0:T(8,128)S(1)}, f32[1,96,256]{2,1,0:T(8,128)}, u32[]{:S(2)}) copy-start(f32[1,96,256]{2,1,0:T(8,128)} %multiply_add_fusion) | copy-start | bytes 294916
  677.9 126.1 %copy-start.6 = (f32[1,256,256]{2,1,0:T(8,128)S(1)}, f32[1,256,256]{2,1,0:T(8,128)}, u32[]{:S(2)}) copy-start(f32[1,256,256]{2,1,0:T(8,128)} %param.12) | copy-start | bytes 786436
Sparse Core Ops, SparseCore 0:
  10.6 54.2 all-gather.4
  68.8 85.3 reduce-scatter.5
  157.7 51.5 all-gather.6
  213.5 85.3 reduce-scatter.7
  451.9 46.4 all-gather.8
  502.2 85.3 reduce-scatter.9
  667.1 47.0 all-gather.10
  718.6 85.3 reduce-scatter.11
where the time goes:
time: 955 us; the launch traced here: 948 us
  waiting for transfers between devices  511 us (54%)
  blocking collectives  363 us (38%)
  matrix products  23.9 us (3%)
  local copies, waits for them, and re-layouts  20.8 us (2%)
  between operations  15.6 us (2%)
  other arithmetic  13.9 us (1%)
    reduce_scatter x4, waiting for transfers between devices, apply_blocks(): lax.psum_scatter(partial_value, 'col', scatter_dimension=0, tiled=True)  339 us
    all_gather x4, waiting for transfers between devices, apply_blocks(): gathered = lax.all_gather(blocks, 'col', axis=0, tiled=True)  171 us
    psum x2, blocking collectives, residual_norm(): return lax.psum(column_dots(residual, residual), ('row', 'col'))  150 us
    unnamed x2, blocking collectives  135 us
    psum x1, blocking collectives, on_device(): curvature = lax.psum(column_dots(direction, images), ('row', 'col'))  77.2 us
  transfers between devices with their start and end apart: 8, of which 8 were waited for; matrix products, arithmetic and copies ran while one was open for 5% of the time, Pallas kernels for 0%

commit v1 on v0

v1 whole, which is shorter than its diff:
```python
import jax
import jax.numpy as jnp
from jax import lax
from jax.experimental import pallas as pl
from jax.experimental.pallas import tpu as pltpu
from jax.sharding import PartitionSpec as P

HIGHEST = lax.Precision.HIGHEST
MESH = pl.DeviceIdType.MESH
F32, BF16, I32 = jnp.float32, jnp.bfloat16, jnp.int32
C, B, K = 96, 256, 7
HALF = C // 2
PLANE, DEPTH, SIDE = 32, 8, 4
NT = (((1,), (1,)), ((), ()))
NN = (((1,), (0,)), ((), ()))
OFFS = (0, -1, 1, 2)
ZERO_BLOCK = PLANE
ZERO_TERM = K
N_AG, N_RS = 35, 20


def split(v):
    high = v.astype(BF16)
    return high, (v - high.astype(F32)).astype(BF16)


def product(v, high_tile, low_tile, dims):
    high, low = split(v)
    both = lax.dot_general(
        jnp.concatenate([high, low], axis=0), high_tile, dims, preferred_element_type=F32
    )
    rest = lax.dot_general(high, low_tile, dims, preferred_element_type=F32)
    return both[: v.shape[0]] + both[v.shape[0] :] + rest


def sums_to_rows(pairs):
    lane = lax.broadcasted_iota(I32, (C, 128), 1)
    wide = jnp.zeros((C, 128), F32)
    for i, (first, second) in enumerate(pairs):
        wide = jnp.where(lane == i, jnp.sum(first * second, axis=1, keepdims=True), wide)
    wide = jnp.concatenate([wide, jnp.zeros((128 - C, 128), F32)], axis=0)
    return jnp.transpose(wide)[0:8]


def rows_to_columns(tile):
    wide = jnp.concatenate([tile, jnp.zeros((120, 128), F32)], axis=0)
    return jnp.transpose(wide)[0:C]


class Place:
    def __init__(self):
        self.row = lax.axis_index("row")
        self.col = lax.axis_index("col")
        col = self.col
        self.core = lax.rem(col, 2)
        x, y = lax.rem(col // 2, SIDE), col // (2 * SIDE)
        core = self.core
        self.a, self.b = x + core * (y - x), y + core * (x - y)
        self.sa, self.sb = 2 + 6 * core, 8 - 6 * core
        self.sibling = col + 1 - 2 * core

    def block(self, da, db):
        return (
            lax.rem(self.a + da + SIDE, SIDE) * self.sa
            + lax.rem(self.b + db + SIDE, SIDE) * self.sb
            + self.core
        )

    def sibling_block(self, da, db):
        return (
            lax.rem(self.b + da + SIDE, SIDE) * self.sb
            + lax.rem(self.a + db + SIDE, SIDE) * self.sa
            + (1 - self.core)
        )


class Gather:
    def __init__(self, place, panel, send_sems, recv_sems):
        self.p, self.panel, self.ss, self.rs = place, panel, send_sems, recv_sems
        self.sent = []

    def copy(self, slot, device, index, half=None):
        part = self.panel.at[slot] if half is None else self.panel.at[slot, pl.ds(half * HALF, HALF)]
        return pltpu.make_async_remote_copy(
            part, part, self.ss.at[index], self.rs.at[index], device_id=(self.p.row, device), device_id_type=MESH
        )

    def send(self, *args):
        copy = self.copy(*args)
        copy.start()
        self.sent.append(copy)

    def wait(self, slot, index, half=None):
        self.copy(slot, self.p.sibling, index, half).wait_recv()

    def along_b(self, i):
        p = self.p
        slot = p.block(OFFS[i], 0)
        self.send(slot, p.block(0, 1), 3 + 2 * i)
        self.send(slot, p.block(0, -1), 4 + 2 * i)
        self.send(slot, p.sibling, 19 + 4 * i)

    def begin(self):
        p = self.p
        for n, da in enumerate((1, -1, 2)):
            self.send(p.col, p.block(da, 0), n)
        self.along_b(0)

    def first(self):
        for i in (1, 2, 3):
            self.wait(self.p.block(OFFS[i], 0), i - 1)
            self.along_b(i)

    def second(self, i):
        p = self.p
        for side, db in ((0, -1), (1, 1)):
            slot = p.block(OFFS[i], db)
            self.wait(slot, 3 + 2 * i + side)
            self.send(slot, p.block(0, -db), 11 + 2 * i + side, side)
            self.send(slot, p.sibling, 20 + 4 * i + side)

    def third(self, i):
        slot = self.p.block(OFFS[i], 2)
        for side in (0, 1):
            self.wait(slot, 11 + 2 * i + side, side)
        self.send(slot, self.p.sibling, 22 + 4 * i)

    def end(self):
        for i in range(SIDE):
            for j in range(SIDE):
                self.wait(self.p.sibling_block(OFFS[i], OFFS[j]), 19 + 4 * i + j)

    def drain(self):
        for copy in self.sent:
            copy.wait_send()


class Scatter:
    def __init__(self, place, term, other, fwd_out, fwd_in, main_out, main_in, last_out, last_in, ss, rs, own, theirs):
        self.p, self.term, self.other = place, term, other
        self.fwd_out, self.fwd_in = fwd_out, fwd_in
        self.main_out, self.main_in = main_out, main_in
        self.last_out, self.last_in = last_out, last_in
        self.ss, self.rs, self.own, self.theirs = ss, rs, own, theirs
        self.sent = []

    def copy(self, src, dst, device, index):
        return pltpu.make_async_remote_copy(
            src, dst, self.ss.at[index], self.rs.at[index], device_id=(self.p.row, device), device_id_type=MESH
        )

    def send(self, *args):
        copy = self.copy(*args)
        copy.start()
        self.sent.append(copy)

    def arrived(self, ref, index):
        self.copy(ref, ref, self.p.sibling, index).wait_recv()

    def begin(self, k):
        self.send(self.term.at[k], self.other.at[k], self.p.sibling, k)

    def terms(self):
        for k in range(K):
            self.arrived(self.other.at[k], k)

    def share(self, da, db):
        block = self.p.block(da, db)
        mine, others = ZERO_TERM, ZERO_TERM
        for k in range(K):
            mine = jnp.where(self.own(k) == block, k, mine)
            others = jnp.where(self.theirs(k) == block, k, others)
        return self.term[mine] + self.other[others]

    def forward(self):
        p = self.p
        for side, da in ((0, 1), (1, -1)):
            for j in (0, 1):
                self.fwd_out[side, j] = self.share(2, OFFS[2 * side + j])
            self.send(self.fwd_out.at[side], self.fwd_in.at[side], p.block(da, 0), K + side)

    def main(self, side, j, extra=None):
        da = 1 - 2 * side
        value = self.share(da, OFFS[j])
        if extra is not None:
            value = value + self.fwd_in[side, extra]
        self.main_out[side, j] = value
        self.send(self.main_out.at[side, j], self.main_in.at[side, j], self.p.block(da, 0), K + 2 + SIDE * side + j)

    def main_free(self):
        for j in (0, 1):
            self.main(0, 2 + j)
            self.main(1, j)

    def main_rest(self):
        for side in (0, 1):
            self.arrived(self.fwd_in.at[side], K + side)
            for j in (0, 1):
                self.main(side, 2 * side + j, j)

    def last(self):
        for j in (2, 1, 3, 0):
            for side in (0, 1):
                self.arrived(self.main_in.at[side, j], K + 2 + SIDE * side + j)
            self.last_out[j] = self.share(0, OFFS[j]) + self.main_in[0, j] + self.main_in[1, j]
            if j:
                self.send(self.last_out.at[j], self.last_in.at[j - 1], self.p.block(0, OFFS[j]), 16 + j)

    def result(self):
        for j in (1, 2, 3):
            self.arrived(self.last_in.at[j - 1], 16 + j)
        return self.last_out[0] + self.last_in[0] + self.last_in[1] + self.last_in[2]

    def drain(self):
        for copy in self.sent:
            copy.wait_send()


class Total:
    def __init__(self, place, source, mid, plane_in, depth_in, sems):
        self.p, self.source, self.mid, self.plane_in, self.depth_in = place, source, mid, plane_in, depth_in
        self.pss, self.prs, self.dss, self.drs = sems

    def plane_copy(self, d):
        p = self.p
        device = lax.rem(p.col + d, PLANE)
        return pltpu.make_async_remote_copy(
            self.source(device), self.plane_in.at[d], self.pss.at[d], self.prs.at[d],
            device_id=(p.row, device), device_id_type=MESH,
        )

    def depth_copy(self, d):
        p = self.p
        return pltpu.make_async_remote_copy(
            self.mid, self.depth_in.at[d], self.dss.at[d], self.drs.at[d],
            device_id=(lax.rem(p.row + d, DEPTH), p.col), device_id_type=MESH,
        )

    def begin(self):
        pl.loop(1, PLANE)(lambda d: self.plane_copy(d).start())

    def middle(self, own):
        pl.loop(1, PLANE)(lambda d: self.plane_copy(d).wait_recv())
        total = own
        for d in range(1, PLANE):
            total = total + self.plane_in[d]
        self.mid[...] = total
        pl.loop(1, DEPTH)(lambda d: self.depth_copy(d).start())

    def end(self):
        pl.loop(1, DEPTH)(lambda d: self.depth_copy(d).wait_recv())
        total = self.mid[...]
        for d in range(1, DEPTH):
            total = total + self.depth_in[d]
        return total

    def drain(self):
        pl.loop(1, PLANE)(lambda d: self.plane_copy(d).wait_send())
        pl.loop(1, DEPTH)(lambda d: self.depth_copy(d).wait_send())


def kernel(
    diag_hbm, pairs_hbm, pattern, newton_diag_hbm, newton_pairs_hbm, warm_hbm, targets,
    out, hess,
    tiles, newton_tiles, xh, xl, nh, nl,
    gw, gr, gq,
    term0, term1, other0, other1,
    fo0, fi0, mo0, mi0, lo0, li0,
    fo1, fi1, mo1, mi1, lo1, li1,
    names_out, names_in, names,
    unit, padded, padded_image, hpad,
    tile0, tile1, mids, plane_in, depth_in,
    load_sems, name_sems,
    ag_ss, ag_rs, rs_ss, rs_rs, pss, prs, dss, drs,
):
    p = Place()
    loads = [
        pltpu.make_async_copy(warm_hbm.at[0], gw.at[p.col], load_sems.at[0]),
        pltpu.make_async_copy(pairs_hbm.at[0], tiles.at[pl.ds(0, K)], load_sems.at[1]),
        pltpu.make_async_copy(diag_hbm.at[0], tiles.at[K], load_sems.at[2]),
        pltpu.make_async_copy(newton_pairs_hbm.at[0], newton_tiles.at[pl.ds(0, K)], load_sems.at[3]),
        pltpu.make_async_copy(newton_diag_hbm.at[0], newton_tiles.at[K], load_sems.at[4]),
    ]
    for load in loads:
        load.start()

    barrier = pltpu.get_barrier_semaphore()

    @pl.loop(1, PLANE)
    def _(d):
        pl.semaphore_signal(barrier, inc=1, device_id=(p.row, lax.rem(p.col + d, PLANE)), device_id_type=MESH)

    @pl.loop(1, DEPTH)
    def _(d):
        pl.semaphore_signal(barrier, inc=1, device_id=(lax.rem(p.row + d, DEPTH), p.col), device_id_type=MESH)

    first_col = p.row * PLANE
    lane = lax.broadcasted_iota(I32, (8, 128), 1)
    table = jnp.full((8, 128), -1, I32)
    for k in range(K):
        table = jnp.where(lane == k, pattern[0, k], table)
    names_out[...] = table
    for g in (gw, gr, gq):
        g[ZERO_BLOCK] = jnp.zeros((C, B), F32)
    for t in (term0, term1, other0, other1):
        t[ZERO_TERM] = jnp.zeros((C, B), F32)

    loads[0].wait()
    pl.semaphore_wait(barrier, PLANE + DEPTH - 2)

    def own(k):
        return pattern[0, k] - first_col

    def theirs(k):
        return names[0, k] - first_col

    def pick(k):
        inside = jnp.clip(pattern[0, k] - first_col, 0, PLANE - 1)
        return jnp.where(pattern[0, k] >= 0, inside, ZERO_BLOCK)

    gathers = [Gather(p, g, ag_ss.at[i], ag_rs.at[i]) for i, g in enumerate((gw, gr, gq))]
    scatters = [
        Scatter(p, term0, other0, fo0, fi0, mo0, mi0, lo0, li0, rs_ss.at[0], rs_rs.at[0], own, theirs),
        Scatter(p, term1, other1, fo1, fi1, mo1, mi1, lo1, li1, rs_ss.at[1], rs_rs.at[1], own, theirs),
    ]

    gathers[0].begin()
    name_copy = pltpu.make_async_remote_copy(
        names_out, names_in, name_sems.at[0], name_sems.at[1], device_id=(p.row, p.sibling), device_id_type=MESH
    )
    name_copy.start()

    loads[1].wait()
    loads[2].wait()
    for k in range(K + 1):
        xh[k], xl[k] = split(tiles[k])

    name_copy.wait()
    name_load = pltpu.make_async_copy(names_in, names, name_sems.at[2])
    name_load.start()

    position = lax.broadcasted_iota(I32, (1, B), 1) + (p.row * PLANE + p.col) * B

    def apply_precision(panel, gather, scatter, aside):
        value = panel[p.col]
        for k in range(K):
            scatter.term[k] = product(value, xh[k], xl[k], NN)
            scatter.begin(k)
        aside()
        gather.first()
        scatter.terms()
        scatter.forward()
        scatter.main_free()
        gather.second(0)
        scatter.main_rest()
        gather.second(1)
        gather.second(2)
        gather.third(0)
        gather.second(3)
        gather.third(1)
        scatter.last()
        gather.third(2)
        gather.third(3)
        total = product(value, xh[K], xl[K], NT)
        gather.end()
        for k in range(K):
            total = total + product(panel[pick(k)], xh[k], xl[k], NT)
        return total + scatter.result()

    def first_aside():
        name_load.wait()

        @pl.loop(0, C)
        def _(c):
            unit[pl.ds(c, 1), :] = (position == targets[c]).astype(F32)

    def second_aside():
        loads[3].wait()
        loads[4].wait()
        for k in range(K + 1):
            nh[k], nl[k] = split(newton_tiles[k])

    residual = unit
    product_w = apply_precision(gw, gathers[0], scatters[0], first_aside)
    gr[p.col] = residual[...] - product_w
    gathers[1].begin()
    gq[p.col] = apply_precision(gr, gathers[1], scatters[1], second_aside)
    gathers[2].begin()

    sums = [
        Total(p, source, mids.at[i], plane_in.at[i], depth_in.at[i], (pss.at[i], prs.at[i], dss.at[i], drs.at[i]))
        for i, source in enumerate((lambda _: tile0, lambda _: tile1, lambda device: hpad.at[device]))
    ]
    r, q = gr[p.col], gq[p.col]
    tile = sums_to_rows([(r, r), (r, q)])
    tile0[...] = tile
    sums[0].begin()
    gathers[2].first()
    gathers[2].second(0)
    sums[0].middle(tile)
    for i in (1, 2, 3):
        gathers[2].second(i)
    for i in range(SIDE):
        gathers[2].third(i)
    first_sums = sums[0].end()
    norm, curve = first_sums[0:1], first_sums[1:2]
    step = norm / curve
    step_c = rows_to_columns(jnp.broadcast_to(step, (8, 128)))[:, 0:1]
    rn = gr[p.col] - step_c * gq[p.col]
    total = 0.5 * product(rn, xh[K], xl[K], NT)
    gathers[2].end()
    for k in range(K):
        block = pick(k)
        total = total + product(gr[block] - step_c * gq[block], xh[k], xl[k], NT)
    tile = sums_to_rows([(rn, rn), (rn, 2.0 * total), (rn, gq[p.col])])
    tile1[...] = tile
    sums[1].begin()
    sums[1].middle(tile)
    second_sums = sums[1].end()
    norm_next, inner, cross = second_sums[0:1], second_sums[1:2], second_sums[2:3]
    beta = norm_next / norm
    curve_next = inner + 2.0 * beta * cross + beta * beta * curve
    step_next = norm_next / curve_next
    rows = lax.broadcasted_iota(I32, (8, 128), 0)
    weights = jnp.where(rows == 0, step + step_next * beta + step_next, step_next * step)
    weights_c = rows_to_columns(weights)
    weight_r, weight_q = weights_c[:, 0:1], weights_c[:, 1:2]

    def estimate(block):
        return gw[block] + weight_r * gr[block] - weight_q * gq[block]

    s = estimate(p.col)
    out[0] = s
    image = jnp.zeros((C, B), F32)
    for k in range(K):
        image = image + product(estimate(pick(k)), nh[k], nl[k], NT)
    diag_image = image + product(s, nh[K], nl[K], NT)
    for j in range(PLANE):
        padded[pl.ds(8 * j, 3)] = s[3 * j : 3 * j + 3]
        padded_image[pl.ds(8 * j, 3)] = image[3 * j : 3 * j + 3]
        padded[pl.ds(8 * j + 3, 5)] = jnp.zeros((5, B), F32)
        padded_image[pl.ds(8 * j + 3, 5)] = jnp.zeros((5, B), F32)
    fill = jnp.zeros((128 - C, B), F32)
    h = lax.dot_general(
        padded[...], jnp.concatenate([diag_image, fill], axis=0), NT, precision=HIGHEST, preferred_element_type=F32
    ) + lax.dot_general(
        padded_image[...], jnp.concatenate([s, fill], axis=0), NT, precision=HIGHEST, preferred_element_type=F32
    )
    for j in range(PLANE):
        hpad[j] = h[8 * j : 8 * j + 8]
    sums[2].begin()
    sums[2].middle(hpad[p.col])
    for g in gathers:
        g.drain()
    for g in scatters:
        g.drain()
    for total in sums[:2]:
        total.drain()
    block_sum = sums[2].end()
    sums[2].drain()
    row_index = lax.broadcasted_iota(I32, (16, 128), 0)
    lane_index = lax.broadcasted_iota(I32, (16, 128), 1)
    chooser = (lane_index == row_index + (C // DEPTH) * p.row).astype(F32)
    picked = lax.dot_general(chooser, block_sum, NT, precision=HIGHEST, preferred_element_type=F32)
    hess[...] = picked[0 : C // DEPTH, 0 : C // PLANE]


def on_device(precision_diag, precision_pairs, pattern_cols, newton_diag, newton_pairs, warm_start, target_rows):
    block = (C, B)
    hbm = pl.BlockSpec(memory_space=pl.ANY)
    smem = pl.BlockSpec(memory_space=pltpu.SMEM)
    vmem = pl.BlockSpec(memory_space=pltpu.VMEM)
    panel = pltpu.VMEM((PLANE + 1,) + block, F32)
    terms = pltpu.VMEM((K + 1,) + block, F32)
    pair_of = pltpu.VMEM((2, 2) + block, F32)
    eight = pltpu.VMEM((2, SIDE) + block, F32)
    steps = [pair_of, pair_of, eight, eight, pltpu.VMEM((SIDE,) + block, F32), pltpu.VMEM((SIDE - 1,) + block, F32)]
    dma = pltpu.SemaphoreType.DMA
    return pl.pallas_call(
        kernel,
        out_shape=(jax.ShapeDtypeStruct((1, C, B), F32), jax.ShapeDtypeStruct((C // DEPTH, C // PLANE), F32)),
        in_specs=[hbm, hbm, smem, hbm, hbm, hbm, smem],
        out_specs=(vmem, vmem),
        scratch_shapes=[
            pltpu.VMEM((K + 1, B, B), F32), pltpu.VMEM((K + 1, B, B), F32),
            pltpu.VMEM((K + 1, B, B), BF16), pltpu.VMEM((K + 1, B, B), BF16),
            pltpu.VMEM((K + 1, B, B), BF16), pltpu.VMEM((K + 1, B, B), BF16),
            panel, panel, panel,
            terms, terms, terms, terms,
            *steps, *steps,
            pltpu.VMEM((8, 128), I32), pltpu.VMEM((8, 128), I32), pltpu.SMEM((8, 128), I32),
            pltpu.VMEM(block, F32), pltpu.VMEM((8 * PLANE, B), F32), pltpu.VMEM((8 * PLANE, B), F32),
            pltpu.VMEM((PLANE, 8, 128), F32),
            pltpu.VMEM((8, 128), F32), pltpu.VMEM((8, 128), F32), pltpu.VMEM((3, 8, 128), F32),
            pltpu.VMEM((3, PLANE, 8, 128), F32), pltpu.VMEM((3, DEPTH, 8, 128), F32),
            dma((5,)), dma((3,)),
            dma((3, N_AG)), dma((3, N_AG)), dma((2, N_RS)), dma((2, N_RS)),
            dma((3, PLANE)), dma((3, PLANE)), dma((3, DEPTH)), dma((3, DEPTH)),
        ],
        compiler_params=pltpu.CompilerParams(
            collective_id=0, has_side_effects=True, vmem_limit_bytes=58 * 2**20
        ),
    )(precision_diag, precision_pairs, pattern_cols, newton_diag, newton_pairs, warm_start, target_rows)


def solution(mesh):
    both = ("row", "col")
    placed = (
        P(both, None, None),
        P(both, None, None, None),
        P(both, None),
        P(both, None, None),
        P(both, None, None, None),
        P(both, None, None),
        P(),
    )
    return jax.shard_map(
        on_device,
        mesh=mesh,
        in_specs=placed,
        out_specs=(P(both, None, None), P("row", "col")),
        check_vma=False,
    )
```

time: 955 us -> 105 us (0.11)
  waiting for transfers between devices: 511 us -> 0 us
  blocking collectives: 363 us -> 0 us
  Pallas kernels: 0 us -> 102 us
  matrix products: 23.9 us -> 0 us
  local copies, waits for them, and re-layouts: 20.8 us -> 2.89 us
  between operations: 15.6 us -> 0.64 us
  other arithmetic: 13.9 us -> 0 us
    reduce_scatter x4 -> x0, waiting for transfers between devices: 339 us -> none  [apply_blocks(): lax.psum_scatter(partial_value, 'col', scatter_dimension=0, tiled=True)]
    psum x3 -> x0, blocking collectives: 228 us -> none  [the longest x2 150 us: residual_norm(): return lax.psum(column_dots(residual, residual), ('row', 'col'))]
    all_gather x4 -> x0, waiting for transfers between devices: 171 us -> none  [apply_blocks(): gathered = lax.all_gather(blocks, 'col', axis=0, tiled=True)]
    unnamed x2 -> x0, blocking collectives: 135 us -> none
    pallas_call x0 -> x1, Pallas kernels: none -> 102 us  [on_device(): pl.pallas_call(kernel, out_shape=(jax.ShapeDtypeStruct((1, C, B), F32), j...]
    dot_general x13 -> x0, matrix products: 23.9 us -> none  [the longest x4 8.91 us: apply_blocks(): jnp.einsum('icb,ikba->ikca', blocks, pair_tiles, precision=HIGHEST)]
    scatter-add x4 -> x0, other arithmetic: 11.6 us -> none  [apply_blocks(): partial_value = jnp.zeros_like(gathered).at[local_cols.reshape(-1)].add(m...]
    gather x4 -> x0, local copies, waits for them, and re-layouts: 9.91 us -> none  [apply_blocks(): picked = jnp.take(gathered, local_cols, axis=0) * weights]
  transfers between devices with their start and end apart: 8 -> 0, of which waited for: 8 -> 0; matrix products, arithmetic and copies ran while one was open for 5% -> 0% of each run, Pallas kernels for 0% -> 0%
where the time goes in v1:
time: 105 us
  Pallas kernels  102 us (97%)
  local copies, waits for them, and re-layouts  2.89 us (3%)
    pallas_call x1, Pallas kernels, on_device(): pl.pallas_call(kernel, out_shape=(jax.ShapeDtypeStruct((1, C, B), F32), j...  102 us

profile of v1, /device:TPU:1, one launch (start us, length us, event | category | flops | bytes accessed | tf_op | source)
XLA Modules:
  0.0 105.2 jit_solution(8575566463929471221)
XLA Ops:
  0.6 101.7 %shard_map.86 = (f32[1,96,256]{2,1,0:T(8,128)}, f32[12,3]{1,0:T(8,128)}) custom-call(f32[1,256,256]{2,1,0:T(8,128)} %diag_hbm.1, f32[1,7,256,256]{3,2,1,0:T(8,128)} %pairs_hbm.1, s32[1,7]{1,0:T(1,128)} %pattern.1, f32[1,256,256]{2,1,0:T(8,128)} %newton_diag_hbm.1, f32[1,7,256,256]{3,2,1,0:T(8,128)} %newton_pairs_hbm.1, f32[1,96,256]{2,1,0:T(8,128)} %warm_hbm.1, ...), custom_call_target="tpu_custom_call" | custom-call | tf_op jit(solution)/shard_map/pallas_call | solution.py:479
  102.3 1.4 %copy.9 = f32[12,3]{0,1:T(4,128)} copy(f32[12,3]{1,0:T(8,128)} %get-tuple-element.3) | data formatting | bytes 288 | tf_op jit(solution)/shard_map/pallas_call | solution.py:479
  103.7 1.5 %copy.11 = f32[1,96,256]{2,1,0:T(8,128)} copy(f32[1,96,256]{2,1,0:T(8,128)} %get-tuple-element.6) | data formatting | bytes 196608

commit v2 on v1

v2 whole, which is shorter than its diff:
```python
import jax
import jax.numpy as jnp
from jax import lax
from jax.experimental import pallas as pl
from jax.experimental.pallas import tpu as pltpu
from jax.sharding import PartitionSpec as P

HIGHEST = lax.Precision.HIGHEST
MESH = pl.DeviceIdType.MESH
F32, BF16, I32 = jnp.float32, jnp.bfloat16, jnp.int32
C, B, K = 96, 256, 7
PARTS = 2
W = C // PARTS
HALF = W // 2
PLANE, DEPTH, SIDE = 32, 8, 4
NT = (((1,), (1,)), ((), ()))
NN = (((1,), (0,)), ((), ()))
OFFS = (0, -1, 1, 2)
ZERO_BLOCK = PLANE
ZERO_TERM = K
N_AG, N_RS = 35, 14


def split(v):
    high = v.astype(BF16)
    return high, (v - high.astype(F32)).astype(BF16)


def product(v, high_tile, low_tile, dims):
    high, low = split(v)
    both = lax.dot_general(
        jnp.concatenate([high, low], axis=0), high_tile, dims, preferred_element_type=F32
    )
    rest = lax.dot_general(high, low_tile, dims, preferred_element_type=F32)
    return both[: v.shape[0]] + both[v.shape[0] :] + rest


def sums_to_rows(parts):
    lane = lax.broadcasted_iota(I32, (W, 128), 1)
    stack = []
    for pairs in parts:
        wide = jnp.zeros((W, 128), F32)
        for i, (first, second) in enumerate(pairs):
            wide = jnp.where(lane == i, jnp.sum(first * second, axis=1, keepdims=True), wide)
        stack.append(wide)
    stack.append(jnp.zeros((128 - C, 128), F32))
    return jnp.transpose(jnp.concatenate(stack, axis=0))[0:8]


def rows_to_columns(tile):
    wide = jnp.concatenate([tile, jnp.zeros((120, 128), F32)], axis=0)
    return jnp.transpose(wide)[0:C]


class Place:
    def __init__(self):
        self.row = lax.axis_index("row")
        self.col = lax.axis_index("col")
        col = self.col
        self.core = lax.rem(col, 2)
        x, y = lax.rem(col // 2, SIDE), col // (2 * SIDE)
        core = self.core
        self.a, self.b = x + core * (y - x), y + core * (x - y)
        self.sa, self.sb = 2 + 6 * core, 8 - 6 * core
        self.sibling = col + 1 - 2 * core

    def block(self, da, db):
        return (
            lax.rem(self.a + da + SIDE, SIDE) * self.sa
            + lax.rem(self.b + db + SIDE, SIDE) * self.sb
            + self.core
        )

    def sibling_block(self, da, db):
        return (
            lax.rem(self.b + da + SIDE, SIDE) * self.sb
            + lax.rem(self.a + db + SIDE, SIDE) * self.sa
            + (1 - self.core)
        )


class Gather:
    def __init__(self, place, panel, send_sems, recv_sems):
        self.p, self.panel, self.ss, self.rs = place, panel, send_sems, recv_sems
        self.sent = []

    def copy(self, slot, device, index, half=None):
        part = self.panel.at[slot] if half is None else self.panel.at[slot, pl.ds(half * HALF, HALF)]
        return pltpu.make_async_remote_copy(
            part, part, self.ss.at[index], self.rs.at[index], device_id=(self.p.row, device), device_id_type=MESH
        )

    def send(self, *args):
        copy = self.copy(*args)
        copy.start()
        self.sent.append(copy)

    def wait(self, slot, index, half=None):
        self.copy(slot, self.p.sibling, index, half).wait_recv()

    def along_b(self, i):
        p = self.p
        slot = p.block(OFFS[i], 0)
        self.send(slot, p.block(0, 1), 3 + 2 * i)
        self.send(slot, p.block(0, -1), 4 + 2 * i)
        self.send(slot, p.sibling, 19 + 4 * i)

    def begin(self):
        p = self.p
        for n, da in enumerate((1, -1, 2)):
            self.send(p.col, p.block(da, 0), n)
        self.along_b(0)

    def first(self):
        for i in (1, 2, 3):
            self.wait(self.p.block(OFFS[i], 0), i - 1)
            self.along_b(i)

    def second(self, i):
        p = self.p
        for side, db in ((0, -1), (1, 1)):
            slot = p.block(OFFS[i], db)
            self.wait(slot, 3 + 2 * i + side)
            self.send(slot, p.block(0, -db), 11 + 2 * i + side, side)
            self.send(slot, p.sibling, 20 + 4 * i + side)

    def third(self, i):
        slot = self.p.block(OFFS[i], 2)
        for side in (0, 1):
            self.wait(slot, 11 + 2 * i + side, side)
        self.send(slot, self.p.sibling, 22 + 4 * i)

    def end(self):
        for i in range(SIDE):
            for j in range(SIDE):
                self.wait(self.p.sibling_block(OFFS[i], OFFS[j]), 19 + 4 * i + j)

    def drain(self):
        for copy in self.sent:
            copy.wait_send()


class Scatter:
    def __init__(self, place, term, other, fwd_out, fwd_in, main_out, main_in, last_out, last_in, ss, rs, own, theirs):
        self.p, self.term, self.other = place, term, other
        self.fwd_out, self.fwd_in = fwd_out, fwd_in
        self.main_out, self.main_in = main_out, main_in
        self.last_out, self.last_in = last_out, last_in
        self.ss, self.rs, self.own, self.theirs = ss, rs, own, theirs
        self.sent = []

    def copy(self, src, dst, device, index):
        return pltpu.make_async_remote_copy(
            src, dst, self.ss.at[index], self.rs.at[index], device_id=(self.p.row, device), device_id_type=MESH
        )

    def send(self, *args):
        copy = self.copy(*args)
        copy.start()
        self.sent.append(copy)

    def arrived(self, ref, index):
        self.copy(ref, ref, self.p.sibling, index).wait_recv()

    def begin(self):
        every = pl.ds(0, K)
        self.send(self.term.at[every], self.other.at[every], self.p.sibling, 0)

    def share(self, da, db):
        block = self.p.block(da, db)
        return self.term[self.own[block]] + self.other[self.theirs[block]]

    def forward(self):
        p = self.p
        self.arrived(self.other.at[pl.ds(0, K)], 0)
        for side, da in ((0, 1), (1, -1)):
            for j in (0, 1):
                self.fwd_out[side, j] = self.share(2, OFFS[2 * side + j])
            self.send(self.fwd_out.at[side], self.fwd_in.at[side], p.block(da, 0), 1 + side)

    def main(self, side, j, extra=None):
        da = 1 - 2 * side
        value = self.share(da, OFFS[j])
        if extra is not None:
            value = value + self.fwd_in[side, extra]
        self.main_out[side, j] = value
        self.send(self.main_out.at[side, j], self.main_in.at[side, j], self.p.block(da, 0), 3 + SIDE * side + j)

    def main_free(self):
        for j in (0, 1):
            self.main(0, 2 + j)
            self.main(1, j)

    def main_rest(self):
        for side in (0, 1):
            self.arrived(self.fwd_in.at[side], 1 + side)
            for j in (0, 1):
                self.main(side, 2 * side + j, j)

    def last(self):
        for j in (2, 1, 3, 0):
            for side in (0, 1):
                self.arrived(self.main_in.at[side, j], 3 + SIDE * side + j)
            self.last_out[j] = self.share(0, OFFS[j]) + self.main_in[0, j] + self.main_in[1, j]
            if j:
                self.send(self.last_out.at[j], self.last_in.at[j - 1], self.p.block(0, OFFS[j]), 10 + j)

    def result(self):
        for j in (1, 2, 3):
            self.arrived(self.last_in.at[j - 1], 10 + j)
        return self.last_out[0] + self.last_in[0] + self.last_in[1] + self.last_in[2]

    def drain(self):
        for copy in self.sent:
            copy.wait_send()


class Total:
    def __init__(self, place, source, mid, plane_in, depth_in, sems):
        self.p, self.source, self.mid, self.plane_in, self.depth_in = place, source, mid, plane_in, depth_in
        self.pss, self.prs, self.dss, self.drs = sems

    def plane_copy(self, d):
        p = self.p
        device = lax.rem(p.col + d, PLANE)
        return pltpu.make_async_remote_copy(
            self.source(device), self.plane_in.at[d], self.pss.at[d], self.prs.at[d],
            device_id=(p.row, device), device_id_type=MESH,
        )

    def depth_copy(self, d):
        p = self.p
        return pltpu.make_async_remote_copy(
            self.mid, self.depth_in.at[d], self.dss.at[d], self.drs.at[d],
            device_id=(lax.rem(p.row + d, DEPTH), p.col), device_id_type=MESH,
        )

    def begin(self):
        pl.loop(1, PLANE)(lambda d: self.plane_copy(d).start())

    def middle(self, own):
        pl.loop(1, PLANE)(lambda d: self.plane_copy(d).wait_recv())
        total = own
        for d in range(1, PLANE):
            total = total + self.plane_in[d]
        self.mid[...] = total
        pl.loop(1, DEPTH)(lambda d: self.depth_copy(d).start())

    def end(self):
        pl.loop(1, DEPTH)(lambda d: self.depth_copy(d).wait_recv())
        total = self.mid[...]
        for d in range(1, DEPTH):
            total = total + self.depth_in[d]
        return total

    def drain(self):
        pl.loop(1, PLANE)(lambda d: self.plane_copy(d).wait_send())
        pl.loop(1, DEPTH)(lambda d: self.depth_copy(d).wait_send())


def kernel(
    diag_hbm, pairs_hbm, pattern, newton_diag_hbm, newton_pairs_hbm, warm_hbm, targets,
    out, hess,
    tiles, newton_tiles, xh, xl, nh, nl,
    gw0, gw1, gr0, gr1, gq0, gq1,
    *refs,
):
    refs = list(refs)
    n_scatter = 2 * PARTS
    buffers = [[refs.pop(0) for _ in range(8)] for _ in range(n_scatter)]
    (
        names_out, names_in, names, own_table, sibling_table,
        unit, padded, padded_image, right, right_image, message,
        tile, tile_mid, message_mid, tile_plane, tile_depth, message_plane, message_depth,
        load_sems, name_sems,
        ag_ss, ag_rs, rs_ss, rs_rs, pss, prs, dss, drs,
    ) = refs
    p = Place()
    loads = [
        pltpu.make_async_copy(warm_hbm.at[0, pl.ds(0, W)], gw0.at[p.col], load_sems.at[0]),
        pltpu.make_async_copy(warm_hbm.at[0, pl.ds(W, W)], gw1.at[p.col], load_sems.at[5]),
        pltpu.make_async_copy(pairs_hbm.at[0], tiles.at[pl.ds(0, K)], load_sems.at[1]),
        pltpu.make_async_copy(diag_hbm.at[0], tiles.at[K], load_sems.at[2]),
        pltpu.make_async_copy(newton_pairs_hbm.at[0], newton_tiles.at[pl.ds(0, K)], load_sems.at[3]),
        pltpu.make_async_copy(newton_diag_hbm.at[0], newton_tiles.at[K], load_sems.at[4]),
    ]
    for load in loads:
        load.start()

    barrier = pltpu.get_barrier_semaphore()

    @pl.loop(1, PLANE)
    def _(d):
        pl.semaphore_signal(barrier, inc=1, device_id=(p.row, lax.rem(p.col + d, PLANE)), device_id_type=MESH)

    @pl.loop(1, DEPTH)
    def _(d):
        pl.semaphore_signal(barrier, inc=1, device_id=(lax.rem(p.row + d, DEPTH), p.col), device_id_type=MESH)

    first_col = p.row * PLANE

    def fill_table(table, source):
        @pl.loop(0, PLANE)
        def _(block):
            at = jnp.int32(ZERO_TERM)
            for k in range(K):
                at = jnp.where(source[0, k] - first_col == block, k, at)
            table[block] = at

    lane = lax.broadcasted_iota(I32, (8, 128), 1)
    table = jnp.full((8, 128), -1, I32)
    for k in range(K):
        table = jnp.where(lane == k, pattern[0, k], table)
    names_out[...] = table
    panels = ((gw0, gw1), (gr0, gr1), (gq0, gq1))
    for pair in panels:
        for g in pair:
            g[ZERO_BLOCK] = jnp.zeros((W, B), F32)
    for group in buffers:
        for t in group[:2]:
            t[ZERO_TERM] = jnp.zeros((W, B), F32)
    fill_table(own_table, pattern)
    position = lax.broadcasted_iota(I32, (1, B), 1) + (p.row * PLANE + p.col) * B

    @pl.loop(0, C)
    def _(c):
        unit[pl.ds(c, 1), :] = (position == targets[c]).astype(F32)

    for load in loads[:4]:
        load.wait()
    for k in range(K + 1):
        xh[k], xl[k] = split(tiles[k])

    pl.semaphore_wait(barrier, PLANE + DEPTH - 2)

    def pick(k):
        inside = jnp.clip(pattern[0, k] - first_col, 0, PLANE - 1)
        return jnp.where(pattern[0, k] >= 0, inside, ZERO_BLOCK)

    gathers = [
        [Gather(p, panels[v][h], ag_ss.at[v * PARTS + h], ag_rs.at[v * PARTS + h]) for h in range(PARTS)]
        for v in range(3)
    ]
    scatters = [
        [
            Scatter(p, *buffers[v * PARTS + h], rs_ss.at[v * PARTS + h], rs_rs.at[v * PARTS + h], own_table, sibling_table)
            for h in range(PARTS)
        ]
        for v in range(2)
    ]

    def begin(v, h):
        gathers[v][h].begin()
        if v < 2:
            scatter = scatters[v][h]
            value = panels[v][h][p.col]
            for k in range(K):
                scatter.term[k] = product(value, xh[k], xl[k], NN)
            scatter.begin()

    def first(v, h):
        if v < 2:
            scatters[v][h].forward()
            scatters[v][h].main_free()
        gathers[v][h].first()

    def second(v, h):
        if v < 2:
            scatters[v][h].main_rest()
        for i in range(SIDE):
            gathers[v][h].second(i)

    def third(v, h):
        if v < 2:
            scatters[v][h].last()
        for i in range(SIDE):
            gathers[v][h].third(i)

    def image(v, h):
        panel = panels[v][h]
        total = lax.dot_general(panel[p.col], tiles[K], NT, precision=HIGHEST, preferred_element_type=F32)
        gathers[v][h].end()
        for k in range(K):
            total = total + product(panel[pick(k)], xh[k], xl[k], NT)
        return total + scatters[v][h].result()

    def residual(h):
        panels[1][h][p.col] = unit[h * W : (h + 1) * W] - image(0, h)

    def q_image(h):
        panels[2][h][p.col] = image(1, h)

    gathers[0][0].begin()
    name_copy = pltpu.make_async_remote_copy(
        names_out, names_in, name_sems.at[0], name_sems.at[1], device_id=(p.row, p.sibling), device_id_type=MESH
    )
    name_copy.start()
    scatter = scatters[0][0]
    value = gw0[p.col]
    for k in range(K):
        scatter.term[k] = product(value, xh[k], xl[k], NN)
    scatter.begin()
    name_copy.wait()
    name_load = pltpu.make_async_copy(names_in, names, name_sems.at[2])
    name_load.start()
    name_load.wait()
    fill_table(sibling_table, names)

    first(0, 0)
    begin(0, 1)
    second(0, 0)
    first(0, 1)
    third(0, 0)
    second(0, 1)
    residual(0)
    begin(1, 0)
    third(0, 1)
    first(1, 0)
    residual(1)
    begin(1, 1)
    second(1, 0)
    first(1, 1)
    third(1, 0)
    loads[4].wait()
    loads[5].wait()
    for k in range(K + 1):
        nh[k], nl[k] = split(newton_tiles[k])
    second(1, 1)
    q_image(0)
    begin(2, 0)
    third(1, 1)
    first(2, 0)
    q_image(1)
    begin(2, 1)

    sums = Total(p, lambda _: tile, tile_mid, tile_plane, tile_depth, (pss.at[0], prs.at[0], dss.at[0], drs.at[0]))
    pairs = []
    for h in range(PARTS):
        r, q = panels[1][h][p.col], panels[2][h][p.col]
        pairs.append([(r, r), (r, q), (q, q)])
    own_sums = sums_to_rows(pairs)
    tile[...] = own_sums
    sums.begin()
    second(2, 0)
    first(2, 1)
    sums.middle(own_sums)
    third(2, 0)
    second(2, 1)
    totals = sums.end()
    norm, curve, square = totals[0:1], totals[1:2], totals[2:3]
    step = norm / curve
    norm_next = step * step * square - 2.0 * step * curve + norm
    beta = norm_next / norm
    rows = lax.broadcasted_iota(I32, (8, 128), 0)
    weights = rows_to_columns(jnp.where(rows == 0, step, beta))

    def weight(h):
        part = weights[h * W : (h + 1) * W]
        return part[:, 0:1], 1.0 + part[:, 1:2]

    def estimate(h, block):
        return gw(h)[block] + weight(h)[0] * gr(h)[block]

    def direction(h, block):
        step_c, scale = weight(h)
        return scale * gr(h)[block] - step_c * gq(h)[block]

    def gw(h):
        return panels[0][h]

    def gr(h):
        return panels[1][h]

    def gq(h):
        return panels[2][h]

    def both_parts(f, block):
        return jnp.concatenate([f(h, block) for h in range(PARTS)], axis=0)

    estimate_image = jnp.zeros((C, B), F32)
    for k in range(K):
        estimate_image = estimate_image + product(both_parts(estimate, pick(k)), nh[k], nl[k], NT)
    u = both_parts(estimate, p.col)
    estimate_full = estimate_image + product(u, nh[K], nl[K], NT)
    third(2, 1)
    for h in range(PARTS):
        gathers[2][h].end()

    d = both_parts(direction, p.col)
    half_image = 0.5 * product(d, xh[K], xl[K], NT)
    direction_image = jnp.zeros((C, B), F32)
    for k in range(K):
        picked = both_parts(direction, pick(k))
        half_image = half_image + product(picked, xh[k], xl[k], NT)
        direction_image = direction_image + product(picked, nh[k], nl[k], NT)
    direction_full = direction_image + product(d, nh[K], nl[K], NT)
    curve_next = sums_to_rows([[(d[h * W : (h + 1) * W], 2.0 * half_image[h * W : (h + 1) * W])] for h in range(PARTS)])

    for j in range(PLANE):
        rows3 = slice(3 * j, 3 * j + 3)
        for ref, first_half, second_half in ((padded, u, d), (padded_image, estimate_image, direction_image)):
            ref[pl.ds(8 * j, 3)] = first_half[rows3]
            ref[pl.ds(8 * j + 3, 3)] = second_half[rows3]
            ref[pl.ds(8 * j + 6, 2)] = jnp.zeros((2, B), F32)
    fill = jnp.zeros((128 - C, B), F32)
    right[...] = jnp.concatenate([u, fill, d, fill], axis=0)
    right_image[...] = jnp.concatenate([estimate_full, fill, direction_full, fill], axis=0)
    pair_sums = lax.dot_general(
        padded[...], right_image[...], NT, precision=HIGHEST, preferred_element_type=F32
    ) + lax.dot_general(padded_image[...], right[...], NT, precision=HIGHEST, preferred_element_type=F32)
    curve_row = jnp.concatenate([curve_next[0:1], jnp.zeros((1, 128), F32)], axis=1)
    row_of = lax.broadcasted_iota(I32, (8, 256), 0)
    for j in range(PLANE):
        message[j] = jnp.where(row_of == 6, curve_row, pair_sums[8 * j : 8 * j + 8])
    last = Total(
        p, lambda device: message.at[device], message_mid, message_plane, message_depth,
        (pss.at[1], prs.at[1], dss.at[1], drs.at[1]),
    )
    last.begin()
    for v in range(3):
        for h in range(PARTS):
            gathers[v][h].drain()
            if v < 2:
                scatters[v][h].drain()
    sums.drain()
    last.middle(message[p.col])
    total = last.end()
    last.drain()
    step_next = norm_next / total[6:7, 0:128]
    spread = rows_to_columns(jnp.broadcast_to(step_next, (8, 128)))
    out[0] = u + spread[:, 0:1] * d
    lane8 = lax.broadcasted_iota(I32, (8, 128), 1)
    row8 = lax.broadcasted_iota(I32, (8, 128), 0)
    mine = lane8 == row8 + (C // PLANE) * p.col
    step_rows = jnp.sum(jnp.where(mine, step_next, 0.0), axis=1, keepdims=True)[0:3]
    block_rows = total[0:3, 0:128] + step_next * total[0:3, 128:256]
    block_rows = block_rows + step_rows * (total[3:6, 0:128] + step_next * total[3:6, 128:256])
    block_rows = jnp.where(lane8[0:3] < C, block_rows, 0.0)
    block_rows = jnp.concatenate([block_rows, jnp.zeros((5, 128), F32)], axis=0)
    row_index = lax.broadcasted_iota(I32, (16, 128), 0)
    lane_index = lax.broadcasted_iota(I32, (16, 128), 1)
    chooser = (lane_index == row_index + (C // DEPTH) * p.row).astype(F32)
    picked = lax.dot_general(chooser, block_rows, NT, precision=HIGHEST, preferred_element_type=F32)
    hess[...] = picked[0 : C // DEPTH, 0 : C // PLANE]


def on_device(precision_diag, precision_pairs, pattern_cols, newton_diag, newton_pairs, warm_start, target_rows):
    block = (W, B)
    hbm = pl.BlockSpec(memory_space=pl.ANY)
    smem = pl.BlockSpec(memory_space=pltpu.SMEM)
    vmem = pl.BlockSpec(memory_space=pltpu.VMEM)
    panel = pltpu.VMEM((PLANE + 1,) + block, F32)
    terms = pltpu.VMEM((K + 1,) + block, F32)
    pair_of = pltpu.VMEM((2, 2) + block, F32)
    eight = pltpu.VMEM((2, SIDE) + block, F32)
    four, three = pltpu.VMEM((SIDE,) + block, F32), pltpu.VMEM((SIDE - 1,) + block, F32)
    scatter = [terms, terms, pair_of, pair_of, eight, eight, four, three]
    square = pltpu.VMEM((8 * PLANE, B), F32)
    tile, message = (8, 128), (8, 256)
    dma = pltpu.SemaphoreType.DMA
    return pl.pallas_call(
        kernel,
        out_shape=(jax.ShapeDtypeStruct((1, C, B), F32), jax.ShapeDtypeStruct((C // DEPTH, C // PLANE), F32)),
        in_specs=[hbm, hbm, smem, hbm, hbm, hbm, smem],
        out_specs=(vmem, vmem),
        scratch_shapes=[
            pltpu.VMEM((K + 1, B, B), F32), pltpu.VMEM((K + 1, B, B), F32),
            pltpu.VMEM((K + 1, B, B), BF16), pltpu.VMEM((K + 1, B, B), BF16),
            pltpu.VMEM((K + 1, B, B), BF16), pltpu.VMEM((K + 1, B, B), BF16),
            *[panel] * (3 * PARTS),
            *scatter * (2 * PARTS),
            pltpu.VMEM((8, 128), I32), pltpu.VMEM((8, 128), I32), pltpu.SMEM((8, 128), I32),
            pltpu.SMEM((PLANE,), I32), pltpu.SMEM((PLANE,), I32),
            pltpu.VMEM((C, B), F32), square, square, square, square,
            pltpu.VMEM((PLANE,) + message, F32),
            pltpu.VMEM(tile, F32), pltpu.VMEM(tile, F32), pltpu.VMEM(message, F32),
            pltpu.VMEM((PLANE,) + tile, F32), pltpu.VMEM((DEPTH,) + tile, F32),
            pltpu.VMEM((PLANE,) + message, F32), pltpu.VMEM((DEPTH,) + message, F32),
            dma((6,)), dma((3,)),
            dma((3 * PARTS, N_AG)), dma((3 * PARTS, N_AG)), dma((2 * PARTS, N_RS)), dma((2 * PARTS, N_RS)),
            dma((2, PLANE)), dma((2, PLANE)), dma((2, DEPTH)), dma((2, DEPTH)),
        ],
        compiler_params=pltpu.CompilerParams(
            collective_id=0, has_side_effects=True, vmem_limit_bytes=58 * 2**20
        ),
    )(precision_diag, precision_pairs, pattern_cols, newton_diag, newton_pairs, warm_start, target_rows)


def solution(mesh):
    both = ("row", "col")
    placed = (
        P(both, None, None),
        P(both, None, None, None),
        P(both, None),
        P(both, None, None),
        P(both, None, None, None),
        P(both, None, None),
        P(),
    )
    return jax.shard_map(
        on_device,
        mesh=mesh,
        in_specs=placed,
        out_specs=(P(both, None, None), P("row", "col")),
        check_vma=False,
    )
```

time: 105 us -> 92 us (0.88)
  Pallas kernels: 102 us -> 88.3 us
    pallas_call x1, Pallas kernels: 102 us -> 88.3 us  [on_device(): pl.pallas_call(kernel, out_shape=(jax.ShapeDtypeStruct((1, C, B), F32), j...]
where the time goes in v2:
time: 92 us; the launch traced here: 91.8 us
  Pallas kernels  88.3 us (96%)
  local copies, waits for them, and re-layouts  2.89 us (3%)
    pallas_call x1, Pallas kernels, on_device(): pl.pallas_call(kernel, out_shape=(jax.ShapeDtypeStruct((1, C, B), F32), j...  88.3 us

profile of v2, /device:TPU:1, one launch (start us, length us, event | category | flops | bytes accessed | tf_op | source)
XLA Modules:
  0.0 91.8 jit_solution(6914944902371535816)
XLA Ops:
  0.6 88.3 %shard_map.86 = (f32[1,96,256]{2,1,0:T(8,128)}, f32[12,3]{1,0:T(8,128)}) custom-call(f32[1,256,256]{2,1,0:T(8,128)} %diag_hbm.1, f32[1,7,256,256]{3,2,1,0:T(8,128)} %pairs_hbm.1, s32[1,7]{1,0:T(1,128)} %pattern.1, f32[1,256,256]{2,1,0:T(8,128)} %newton_diag_hbm.1, f32[1,7,256,256]{3,2,1,0:T(8,128)} %newton_pairs_hbm.1, f32[1,96,256]{2,1,0:T(8,128)} %warm_hbm.1, ...), custom_call_target="tpu_custom_call" | custom-call | tf_op jit(solution)/shard_map/pallas_call | solution.py:561
  88.9 1.4 %copy.9 = f32[12,3]{0,1:T(4,128)} copy(f32[12,3]{1,0:T(8,128)} %get-tuple-element.3) | data formatting | bytes 288 | tf_op jit(solution)/shard_map/pallas_call | solution.py:561
  90.3 1.5 %copy.11 = f32[1,96,256]{2,1,0:T(8,128)} copy(f32[1,96,256]{2,1,0:T(8,128)} %get-tuple-element.6) | data formatting | bytes 196608

commit v3 on v2

--- a/solution.py
+++ b/solution.py
@@ -18,7 +18,7 @@
 OFFS = (0, -1, 1, 2)
 ZERO_BLOCK = PLANE
 ZERO_TERM = K
-N_AG, N_RS = 35, 14
+N_AG, N_RS = 12, 7
 
 
 def split(v):
@@ -35,16 +35,17 @@
     return both[: v.shape[0]] + both[v.shape[0] :] + rest
 
 
-def sums_to_rows(parts):
-    lane = lax.broadcasted_iota(I32, (W, 128), 1)
-    stack = []
-    for pairs in parts:
-        wide = jnp.zeros((W, 128), F32)
-        for i, (first, second) in enumerate(pairs):
-            wide = jnp.where(lane == i, jnp.sum(first * second, axis=1, keepdims=True), wide)
-        stack.append(wide)
-    stack.append(jnp.zeros((128 - C, 128), F32))
-    return jnp.transpose(jnp.concatenate(stack, axis=0))[0:8]
+def side_sums(pairs):
+    n = pairs[0][0].shape[0]
+    lane = lax.broadcasted_iota(I32, (n, 128), 1)
+    wide = jnp.zeros((n, 128), F32)
+    for i, (first, second) in enumerate(pairs):
+        wide = jnp.where(lane == i, jnp.sum(first * second, axis=1, keepdims=True), wide)
+    return wide
+
+
+def stack_to_rows(stack):
+    return jnp.transpose(jnp.concatenate(stack + [jnp.zeros((128 - C, 128), F32)], axis=0))[0:8]
 
 
 def rows_to_columns(tile):
@@ -80,30 +81,27 @@
 
 
 class Gather:
-    def __init__(self, place, panel, send_sems, recv_sems):
-        self.p, self.panel, self.ss, self.rs = place, panel, send_sems, recv_sems
-        self.sent = []
-
-    def copy(self, slot, device, index, half=None):
+    def __init__(self, place, panel, send_sem, recv_sems):
+        self.p, self.panel, self.ss, self.rs = place, panel, send_sem, recv_sems
+
+    def copy(self, part, device, index):
+        return pltpu.make_async_remote_copy(
+            part, part, self.ss, self.rs.at[index], device_id=(self.p.row, device), device_id_type=MESH
+        )
+
+    def send(self, slot, device, index, half=None):
         part = self.panel.at[slot] if half is None else self.panel.at[slot, pl.ds(half * HALF, HALF)]
-        return pltpu.make_async_remote_copy(
-            part, part, self.ss.at[index], self.rs.at[index], device_id=(self.p.row, device), device_id_type=MESH
-        )
-
-    def send(self, *args):
-        copy = self.copy(*args)
-        copy.start()
-        self.sent.append(copy)
-
-    def wait(self, slot, index, half=None):
-        self.copy(slot, self.p.sibling, index, half).wait_recv()
+        self.copy(part, device, index).start()
+
+    def wait(self, index, blocks):
+        self.copy(self.panel.at[pl.ds(0, blocks)], self.p.sibling, index).wait_recv()
 
     def along_b(self, i):
         p = self.p
         slot = p.block(OFFS[i], 0)
-        self.send(slot, p.block(0, 1), 3 + 2 * i)
-        self.send(slot, p.block(0, -1), 4 + 2 * i)
-        self.send(slot, p.sibling, 19 + 4 * i)
+        self.send(slot, p.block(0, 1), 3 + i)
+        self.send(slot, p.block(0, -1), 3 + i)
+        self.send(slot, p.sibling, 11)
 
     def begin(self):
         p = self.p
@@ -113,53 +111,46 @@
 
     def first(self):
         for i in (1, 2, 3):
-            self.wait(self.p.block(OFFS[i], 0), i - 1)
+            self.wait(i - 1, 1)
             self.along_b(i)
 
     def second(self, i):
         p = self.p
-        for side, db in ((0, -1), (1, 1)):
-            slot = p.block(OFFS[i], db)
-            self.wait(slot, 3 + 2 * i + side)
-            self.send(slot, p.block(0, -db), 11 + 2 * i + side, side)
-            self.send(slot, p.sibling, 20 + 4 * i + side)
+        self.wait(3 + i, 2)
+        for half, db in ((0, -1), (1, 1)):
+            self.send(p.block(OFFS[i], db), p.block(0, -db), 7 + i, half)
+        for db in (-1, 1):
+            self.send(p.block(OFFS[i], db), p.sibling, 11)
 
     def third(self, i):
-        slot = self.p.block(OFFS[i], 2)
-        for side in (0, 1):
-            self.wait(slot, 11 + 2 * i + side, side)
-        self.send(slot, self.p.sibling, 22 + 4 * i)
+        self.wait(7 + i, 1)
+        self.send(self.p.block(OFFS[i], 2), self.p.sibling, 11)
 
     def end(self):
-        for i in range(SIDE):
-            for j in range(SIDE):
-                self.wait(self.p.sibling_block(OFFS[i], OFFS[j]), 19 + 4 * i + j)
+        self.wait(11, SIDE * SIDE)
 
     def drain(self):
-        for copy in self.sent:
-            copy.wait_send()
+        sent = 3 + 2 * SIDE + SIDE + SIDE * SIDE
+        self.copy(self.panel.at[pl.ds(0, sent)], self.p.sibling, 11).wait_send()
 
 
 class Scatter:
-    def __init__(self, place, term, other, fwd_out, fwd_in, main_out, main_in, last_out, last_in, ss, rs, own, theirs):
-        self.p, self.term, self.other = place, term, other
+    def __init__(self, place, panel, term, other, fwd_out, fwd_in, main_out, main_in, last_out, last_in, ss, rs, own, theirs):
+        self.p, self.panel, self.term, self.other = place, panel, term, other
         self.fwd_out, self.fwd_in = fwd_out, fwd_in
         self.main_out, self.main_in = main_out, main_in
         self.last_out, self.last_in = last_out, last_in
         self.ss, self.rs, self.own, self.theirs = ss, rs, own, theirs
-        self.sent = []
 
     def copy(self, src, dst, device, index):
         return pltpu.make_async_remote_copy(
-            src, dst, self.ss.at[index], self.rs.at[index], device_id=(self.p.row, device), device_id_type=MESH
+            src, dst, self.ss, self.rs.at[index], device_id=(self.p.row, device), device_id_type=MESH
         )
 
     def send(self, *args):
-        copy = self.copy(*args)
-        copy.start()
-        self.sent.append(copy)
-
-    def arrived(self, ref, index):
+        self.copy(*args).start()
+
+    def wait(self, ref, index):
         self.copy(ref, ref, self.p.sibling, index).wait_recv()
 
     def begin(self):
@@ -171,20 +162,19 @@
         return self.term[self.own[block]] + self.other[self.theirs[block]]
 
     def forward(self):
-        p = self.p
-        self.arrived(self.other.at[pl.ds(0, K)], 0)
+        self.wait(self.other.at[pl.ds(0, K)], 0)
         for side, da in ((0, 1), (1, -1)):
             for j in (0, 1):
                 self.fwd_out[side, j] = self.share(2, OFFS[2 * side + j])
-            self.send(self.fwd_out.at[side], self.fwd_in.at[side], p.block(da, 0), 1 + side)
+            self.send(self.fwd_out.at[side], self.fwd_in.at[side], self.p.block(da, 0), 1)
 
     def main(self, side, j, extra=None):
         da = 1 - 2 * side
         value = self.share(da, OFFS[j])
         if extra is not None:
             value = value + self.fwd_in[side, extra]
-        self.main_out[side, j] = value
-        self.send(self.main_out.at[side, j], self.main_in.at[side, j], self.p.block(da, 0), 3 + SIDE * side + j)
+        self.main_out[j, side] = value
+        self.send(self.main_out.at[j, side], self.main_in.at[j, side], self.p.block(da, 0), 2 + j)
 
     def main_free(self):
         for j in (0, 1):
@@ -192,27 +182,26 @@
             self.main(1, j)
 
     def main_rest(self):
-        for side in (0, 1):
-            self.arrived(self.fwd_in.at[side], 1 + side)
-            for j in (0, 1):
-                self.main(side, 2 * side + j, j)
+        self.wait(self.fwd_in, 1)
+        for j in (0, 1):
+            self.main(0, j, j)
+            self.main(1, 2 + j, j)
 
     def last(self):
-        for j in (2, 1, 3, 0):
-            for side in (0, 1):
-                self.arrived(self.main_in.at[side, j], 3 + SIDE * side + j)
-            self.last_out[j] = self.share(0, OFFS[j]) + self.main_in[0, j] + self.main_in[1, j]
+        for j in (3, 1, 2, 0):
+            self.wait(self.main_in.at[j], 2 + j)
+            self.last_out[j] = self.share(0, OFFS[j]) + self.main_in[j, 0] + self.main_in[j, 1]
             if j:
-                self.send(self.last_out.at[j], self.last_in.at[j - 1], self.p.block(0, OFFS[j]), 10 + j)
+                self.send(self.last_out.at[j], self.last_in.at[j - 1], self.p.block(0, OFFS[j]), 6)
 
     def result(self):
-        for j in (1, 2, 3):
-            self.arrived(self.last_in.at[j - 1], 10 + j)
+        self.wait(self.last_in, 6)
         return self.last_out[0] + self.last_in[0] + self.last_in[1] + self.last_in[2]
 
     def drain(self):
-        for copy in self.sent:
-            copy.wait_send()
+        sent = K + 4 + 2 * SIDE + SIDE - 1
+        part = self.panel.at[pl.ds(0, sent)]
+        self.copy(part, part, self.p.sibling, 6).wait_send()
 
 
 class Total:
@@ -224,22 +213,34 @@
         p = self.p
         device = lax.rem(p.col + d, PLANE)
         return pltpu.make_async_remote_copy(
-            self.source(device), self.plane_in.at[d], self.pss.at[d], self.prs.at[d],
+            self.source(device), self.plane_in.at[d], self.pss, self.prs,
             device_id=(p.row, device), device_id_type=MESH,
         )
 
     def depth_copy(self, d):
         p = self.p
         return pltpu.make_async_remote_copy(
-            self.mid, self.depth_in.at[d], self.dss.at[d], self.drs.at[d],
+            self.mid, self.depth_in.at[d], self.dss, self.drs,
             device_id=(lax.rem(p.row + d, DEPTH), p.col), device_id_type=MESH,
         )
 
     def begin(self):
         pl.loop(1, PLANE)(lambda d: self.plane_copy(d).start())
 
+    def whole(self, ref, count, send_sem, recv_sem):
+        part = ref.at[pl.ds(1, count - 1)]
+        return pltpu.make_async_remote_copy(
+            part, part, send_sem, recv_sem, device_id=(self.p.row, self.p.sibling), device_id_type=MESH
+        )
+
+    def plane_whole(self):
+        return self.whole(self.plane_in, PLANE, self.pss, self.prs)
+
+    def depth_whole(self):
+        return self.whole(self.depth_in, DEPTH, self.dss, self.drs)
+
     def middle(self, own):
-        pl.loop(1, PLANE)(lambda d: self.plane_copy(d).wait_recv())
+        self.plane_whole().wait_recv()
         total = own
         for d in range(1, PLANE):
             total = total + self.plane_in[d]
@@ -247,15 +248,15 @@
         pl.loop(1, DEPTH)(lambda d: self.depth_copy(d).start())
 
     def end(self):
-        pl.loop(1, DEPTH)(lambda d: self.depth_copy(d).wait_recv())
+        self.depth_whole().wait_recv()
         total = self.mid[...]
         for d in range(1, DEPTH):
             total = total + self.depth_in[d]
         return total
 
     def drain(self):
-        pl.loop(1, PLANE)(lambda d: self.plane_copy(d).wait_send())
-        pl.loop(1, DEPTH)(lambda d: self.depth_copy(d).wait_send())
+        self.plane_whole().wait_send()
+        self.depth_whole().wait_send()
 
 
 def kernel(
@@ -276,6 +277,16 @@
         ag_ss, ag_rs, rs_ss, rs_rs, pss, prs, dss, drs,
     ) = refs
     p = Place()
+    barrier = pltpu.get_barrier_semaphore()
+
+    @pl.loop(1, PLANE)
+    def _(d):
+        pl.semaphore_signal(barrier, inc=1, device_id=(p.row, lax.rem(p.col + d, PLANE)), device_id_type=MESH)
+
+    @pl.loop(1, DEPTH)
+    def _(d):
+        pl.semaphore_signal(barrier, inc=1, device_id=(lax.rem(p.row + d, DEPTH), p.col), device_id_type=MESH)
+
     loads = [
         pltpu.make_async_copy(warm_hbm.at[0, pl.ds(0, W)], gw0.at[p.col], load_sems.at[0]),
         pltpu.make_async_copy(warm_hbm.at[0, pl.ds(W, W)], gw1.at[p.col], load_sems.at[5]),
@@ -287,16 +298,6 @@
     for load in loads:
         load.start()
 
-    barrier = pltpu.get_barrier_semaphore()
-
-    @pl.loop(1, PLANE)
-    def _(d):
-        pl.semaphore_signal(barrier, inc=1, device_id=(p.row, lax.rem(p.col + d, PLANE)), device_id_type=MESH)
-
-    @pl.loop(1, DEPTH)
-    def _(d):
-        pl.semaphore_signal(barrier, inc=1, device_id=(lax.rem(p.row + d, DEPTH), p.col), device_id_type=MESH)
-
     first_col = p.row * PLANE
 
     def fill_table(table, source):
@@ -313,24 +314,8 @@
         table = jnp.where(lane == k, pattern[0, k], table)
     names_out[...] = table
     panels = ((gw0, gw1), (gr0, gr1), (gq0, gq1))
-    for pair in panels:
-        for g in pair:
-            g[ZERO_BLOCK] = jnp.zeros((W, B), F32)
-    for group in buffers:
-        for t in group[:2]:
-            t[ZERO_TERM] = jnp.zeros((W, B), F32)
-    fill_table(own_table, pattern)
-    position = lax.broadcasted_iota(I32, (1, B), 1) + (p.row * PLANE + p.col) * B
-
-    @pl.loop(0, C)
-    def _(c):
-        unit[pl.ds(c, 1), :] = (position == targets[c]).astype(F32)
-
-    for load in loads[:4]:
-        load.wait()
-    for k in range(K + 1):
-        xh[k], xl[k] = split(tiles[k])
-
+    loads[0].wait()
+    loads[1].wait()
     pl.semaphore_wait(barrier, PLANE + DEPTH - 2)
 
     def pick(k):
@@ -343,7 +328,7 @@
     ]
     scatters = [
         [
-            Scatter(p, *buffers[v * PARTS + h], rs_ss.at[v * PARTS + h], rs_rs.at[v * PARTS + h], own_table, sibling_table)
+            Scatter(p, panels[v][h], *buffers[v * PARTS + h], rs_ss.at[v * PARTS + h], rs_rs.at[v * PARTS + h], own_table, sibling_table)
             for h in range(PARTS)
         ]
         for v in range(2)
@@ -390,16 +375,52 @@
     def q_image(h):
         panels[2][h][p.col] = image(1, h)
 
+    def both_parts(f, block):
+        return jnp.concatenate([f(h, block) for h in range(PARTS)], axis=0)
+
+    def make_units():
+        position = lax.broadcasted_iota(I32, (1, B), 1) + (p.row * PLANE + p.col) * B
+
+        @pl.loop(0, C)
+        def _(c):
+            unit[pl.ds(c, 1), :] = (position == targets[c]).astype(F32)
+
+    def split_newton():
+        loads[4].wait()
+        loads[5].wait()
+        for k in range(K + 1):
+            nh[k], nl[k] = split(newton_tiles[k])
+
+    stacks = []
+
+    def own_sums_of(h):
+        r, q = panels[1][h][p.col], panels[2][h][p.col]
+        stacks.append(side_sums([(r, r), (r, q), (q, q)]))
+
     gathers[0][0].begin()
     name_copy = pltpu.make_async_remote_copy(
         names_out, names_in, name_sems.at[0], name_sems.at[1], device_id=(p.row, p.sibling), device_id_type=MESH
     )
     name_copy.start()
-    scatter = scatters[0][0]
-    value = gw0[p.col]
+    gathers[0][1].begin()
+    loads[2].wait()
+    value = both_parts(lambda h, block: panels[0][h][block], p.col)
     for k in range(K):
-        scatter.term[k] = product(value, xh[k], xl[k], NN)
-    scatter.begin()
+        xh[k], xl[k] = split(tiles[k])
+        term = product(value, xh[k], xl[k], NN)
+        for h in range(PARTS):
+            scatters[0][h].term[k] = term[h * W : (h + 1) * W]
+    for h in range(PARTS):
+        scatters[0][h].begin()
+    loads[3].wait()
+    xh[K], xl[K] = split(tiles[K])
+    for pair in panels:
+        for g in pair:
+            g[ZERO_BLOCK] = jnp.zeros((W, B), F32)
+    for group in buffers:
+        for t in group[:2]:
+            t[ZERO_TERM] = jnp.zeros((W, B), F32)
+    fill_table(own_table, pattern)
     name_copy.wait()
     name_load = pltpu.make_async_copy(names_in, names, name_sems.at[2])
     name_load.start()
@@ -407,9 +428,9 @@
     fill_table(sibling_table, names)
 
     first(0, 0)
-    begin(0, 1)
+    first(0, 1)
     second(0, 0)
-    first(0, 1)
+    make_units()
     third(0, 0)
     second(0, 1)
     residual(0)
@@ -420,25 +441,20 @@
     begin(1, 1)
     second(1, 0)
     first(1, 1)
+    split_newton()
     third(1, 0)
-    loads[4].wait()
-    loads[5].wait()
-    for k in range(K + 1):
-        nh[k], nl[k] = split(newton_tiles[k])
     second(1, 1)
     q_image(0)
     begin(2, 0)
     third(1, 1)
     first(2, 0)
+    own_sums_of(0)
     q_image(1)
     begin(2, 1)
 
     sums = Total(p, lambda _: tile, tile_mid, tile_plane, tile_depth, (pss.at[0], prs.at[0], dss.at[0], drs.at[0]))
-    pairs = []
-    for h in range(PARTS):
-        r, q = panels[1][h][p.col], panels[2][h][p.col]
-        pairs.append([(r, r), (r, q), (q, q)])
-    own_sums = sums_to_rows(pairs)
+    own_sums_of(1)
+    own_sums = stack_to_rows(stacks)
     tile[...] = own_sums
     sums.begin()
     second(2, 0)
@@ -446,6 +462,7 @@
     sums.middle(own_sums)
     third(2, 0)
     second(2, 1)
+    third(2, 1)
     totals = sums.end()
     norm, curve, square = totals[0:1], totals[1:2], totals[2:3]
     step = norm / curve
@@ -474,15 +491,11 @@
     def gq(h):
         return panels[2][h]
 
-    def both_parts(f, block):
-        return jnp.concatenate([f(h, block) for h in range(PARTS)], axis=0)
-
     estimate_image = jnp.zeros((C, B), F32)
     for k in range(K):
         estimate_image = estimate_image + product(both_parts(estimate, pick(k)), nh[k], nl[k], NT)
     u = both_parts(estimate, p.col)
     estimate_full = estimate_image + product(u, nh[K], nl[K], NT)
-    third(2, 1)
     for h in range(PARTS):
         gathers[2][h].end()
 
@@ -494,7 +507,7 @@
         half_image = half_image + product(picked, xh[k], xl[k], NT)
         direction_image = direction_image + product(picked, nh[k], nl[k], NT)
     direction_full = direction_image + product(d, nh[K], nl[K], NT)
-    curve_next = sums_to_rows([[(d[h * W : (h + 1) * W], 2.0 * half_image[h * W : (h + 1) * W])] for h in range(PARTS)])
+    curve_next = stack_to_rows([side_sums([(d, 2.0 * half_image)])])
 
     for j in range(PLANE):
         rows3 = slice(3 * j, 3 * j + 3)
@@ -552,7 +565,7 @@
     panel = pltpu.VMEM((PLANE + 1,) + block, F32)
     terms = pltpu.VMEM((K + 1,) + block, F32)
     pair_of = pltpu.VMEM((2, 2) + block, F32)
-    eight = pltpu.VMEM((2, SIDE) + block, F32)
+    eight = pltpu.VMEM((SIDE, 2) + block, F32)
     four, three = pltpu.VMEM((SIDE,) + block, F32), pltpu.VMEM((SIDE - 1,) + block, F32)
     scatter = [terms, terms, pair_of, pair_of, eight, eight, four, three]
     square = pltpu.VMEM((8 * PLANE, B), F32)
@@ -577,8 +590,8 @@
             pltpu.VMEM((PLANE,) + tile, F32), pltpu.VMEM((DEPTH,) + tile, F32),
             pltpu.VMEM((PLANE,) + message, F32), pltpu.VMEM((DEPTH,) + message, F32),
             dma((6,)), dma((3,)),
-            dma((3 * PARTS, N_AG)), dma((3 * PARTS, N_AG)), dma((2 * PARTS, N_RS)), dma((2 * PARTS, N_RS)),
-            dma((2, PLANE)), dma((2, PLANE)), dma((2, DEPTH)), dma((2, DEPTH)),
+            dma((3 * PARTS,)), dma((3 * PARTS, N_AG)), dma((2 * PARTS,)), dma((2 * PARTS, N_RS)),
+            dma((2,)), dma((2,)), dma((2,)), dma((2,)),
         ],
         compiler_params=pltpu.CompilerParams(
             collective_id=0, has_side_effects=True, vmem_limit_bytes=58 * 2**20

time: 92 us -> 86.7 us (0.942)
  Pallas kernels: 88.3 us -> 83 us
    pallas_call x1, Pallas kernels: 88.3 us -> 83 us  [on_device(): pl.pallas_call(kernel, out_shape=(jax.ShapeDtypeStruct((1, C, B), F32), j...]
where the time goes in v3:
time: 86.7 us; the launch traced here: 86.5 us
  Pallas kernels  83 us (96%)
  local copies, waits for them, and re-layouts  2.89 us (3%)
    pallas_call x1, Pallas kernels, on_device(): pl.pallas_call(kernel, out_shape=(jax.ShapeDtypeStruct((1, C, B), F32), j...  83 us

profile of v3, /device:TPU:1, one launch (start us, length us, event | category | flops | bytes accessed | tf_op | source)
XLA Modules:
  0.0 86.5 jit_solution(17969175722935919224)
XLA Ops:
  0.6 83.0 %shard_map.86 = (f32[1,96,256]{2,1,0:T(8,128)}, f32[12,3]{1,0:T(8,128)}) custom-call(f32[1,256,256]{2,1,0:T(8,128)} %diag_hbm.1, f32[1,7,256,256]{3,2,1,0:T(8,128)} %pairs_hbm.1, s32[1,7]{1,0:T(1,128)} %pattern.1, f32[1,256,256]{2,1,0:T(8,128)} %newton_diag_hbm.1, f32[1,7,256,256]{3,2,1,0:T(8,128)} %newton_pairs_hbm.1, f32[1,96,256]{2,1,0:T(8,128)} %warm_hbm.1, ...), custom_call_target="tpu_custom_call" | custom-call | tf_op jit(solution)/shard_map/pallas_call | solution.py:574
  83.6 1.4 %copy.9 = f32[12,3]{0,1:T(4,128)} copy(f32[12,3]{1,0:T(8,128)} %get-tuple-element.3) | data formatting | bytes 288 | tf_op jit(solution)/shard_map/pallas_call | solution.py:574
  85.0 1.5 %copy.11 = f32[1,96,256]{2,1,0:T(8,128)} copy(f32[1,96,256]{2,1,0:T(8,128)} %get-tuple-element.6) | data formatting | bytes 196608

commit v4 on v3

--- a/solution.py
+++ b/solution.py
@@ -19,6 +19,7 @@
 ZERO_BLOCK = PLANE
 ZERO_TERM = K
 N_AG, N_RS = 12, 7
+STRAIGHT = ((2, 1),)
 
 
 def split(v):
@@ -81,7 +82,8 @@
 
 
 class Gather:
-    def __init__(self, place, panel, send_sem, recv_sems):
+    def __init__(self, place, panel, straight, send_sem, recv_sems):
+        self.straight = straight
         self.p, self.panel, self.ss, self.rs = place, panel, send_sem, recv_sems
 
     def copy(self, part, device, index):
@@ -101,6 +103,8 @@
         slot = p.block(OFFS[i], 0)
         self.send(slot, p.block(0, 1), 3 + i)
         self.send(slot, p.block(0, -1), 3 + i)
+        if self.straight:
+            self.send(slot, p.block(0, 2), 7 + i)
         self.send(slot, p.sibling, 11)
 
     def begin(self):
@@ -117,7 +121,7 @@
     def second(self, i):
         p = self.p
         self.wait(3 + i, 2)
-        for half, db in ((0, -1), (1, 1)):
+        for half, db in () if self.straight else ((0, -1), (1, 1)):
             self.send(p.block(OFFS[i], db), p.block(0, -db), 7 + i, half)
         for db in (-1, 1):
             self.send(p.block(OFFS[i], db), p.sibling, 11)
@@ -323,7 +327,7 @@
         return jnp.where(pattern[0, k] >= 0, inside, ZERO_BLOCK)
 
     gathers = [
-        [Gather(p, panels[v][h], ag_ss.at[v * PARTS + h], ag_rs.at[v * PARTS + h]) for h in range(PARTS)]
+        [Gather(p, panels[v][h], (v, h) in STRAIGHT, ag_ss.at[v * PARTS + h], ag_rs.at[v * PARTS + h]) for h in range(PARTS)]
         for v in range(3)
     ]
     scatters = [
@@ -553,8 +557,13 @@
     row_index = lax.broadcasted_iota(I32, (16, 128), 0)
     lane_index = lax.broadcasted_iota(I32, (16, 128), 1)
     chooser = (lane_index == row_index + (C // DEPTH) * p.row).astype(F32)
-    picked = lax.dot_general(chooser, block_rows, NT, precision=HIGHEST, preferred_element_type=F32)
-    hess[...] = picked[0 : C // DEPTH, 0 : C // PLANE]
+    picked = lax.dot_general(block_rows, chooser, NT, precision=HIGHEST, preferred_element_type=F32)
+    hess[...] = picked[0 : C // PLANE, 0 : C // DEPTH]
+
+
+def hand_over(panel_in, hess_in, panel_out, hess_out):
+    panel_out[...] = panel_in[...]
+    hess_out[...] = hess_in[...]
 
 
 def on_device(precision_diag, precision_pairs, pattern_cols, newton_diag, newton_pairs, warm_start, target_rows):
@@ -571,9 +580,9 @@
     square = pltpu.VMEM((8 * PLANE, B), F32)
     tile, message = (8, 128), (8, 256)
     dma = pltpu.SemaphoreType.DMA
-    return pl.pallas_call(
+    panel_out, hessian = pl.pallas_call(
         kernel,
-        out_shape=(jax.ShapeDtypeStruct((1, C, B), F32), jax.ShapeDtypeStruct((C // DEPTH, C // PLANE), F32)),
+        out_shape=(jax.ShapeDtypeStruct((1, C, B), F32), jax.ShapeDtypeStruct((C // PLANE, C // DEPTH), F32)),
         in_specs=[hbm, hbm, smem, hbm, hbm, hbm, smem],
         out_specs=(vmem, vmem),
         scratch_shapes=[
@@ -597,6 +606,13 @@
             collective_id=0, has_side_effects=True, vmem_limit_bytes=58 * 2**20
         ),
     )(precision_diag, precision_pairs, pattern_cols, newton_diag, newton_pairs, warm_start, target_rows)
+    panel_out, hessian = pl.pallas_call(
+        hand_over,
+        out_shape=(jax.ShapeDtypeStruct((1, C, B), F32), jax.ShapeDtypeStruct((C // PLANE, C // DEPTH), F32)),
+        in_specs=[vmem, vmem],
+        out_specs=(vmem, vmem),
+    )(panel_out, hessian)
+    return panel_out, hessian.T
 
 
 def solution(mesh):

time: 86.7 us -> 84.7 us (0.977)
  local copies, waits for them, and re-layouts: 2.89 us -> 0 us
  Pallas kernels: 83 us -> 83.9 us
    pallas_call x0 -> x1, Pallas kernels: none -> 1.55 us  [on_device(): pl.pallas_call(hand_over, out_shape=(jax.ShapeDtypeStruct((1, C, B), F32)...]
    unnamed x1 -> x0, local copies, waits for them, and re-layouts: 1.54 us -> none
    pallas_call x1 -> x0, local copies, waits for them, and re-layouts: 1.35 us -> none  [on_device(): pl.pallas_call(kernel, out_shape=(jax.ShapeDtypeStruct((1, C, B), F32), j...]
where the time goes in v4:
time: 84.7 us; the launch traced here: 84.5 us
  Pallas kernels  83.9 us (99%)
    pallas_call x1, Pallas kernels, on_device(): pl.pallas_call(kernel, out_shape=(jax.ShapeDtypeStruct((1, C, B), F32), j...  82.3 us

profile of v4, /device:TPU:1, one launch (start us, length us, event | category | flops | bytes accessed | tf_op | source)
XLA Modules:
  0.0 84.5 jit_solution(10287387428765280067)
XLA Ops:
  0.6 82.3 %shard_map.86 = (f32[1,96,256]{2,1,0:T(8,128)}, f32[3,12]{1,0:T(4,128)}) custom-call(f32[1,256,256]{2,1,0:T(8,128)} %diag_hbm.1, f32[1,7,256,256]{3,2,1,0:T(8,128)} %pairs_hbm.1, s32[1,7]{1,0:T(1,128)} %pattern.1, f32[1,256,256]{2,1,0:T(8,128)} %newton_diag_hbm.1, f32[1,7,256,256]{3,2,1,0:T(8,128)} %newton_pairs_hbm.1, f32[1,96,256]{2,1,0:T(8,128)} %warm_hbm.1, ...), custom_call_target="tpu_custom_call" | custom-call | tf_op jit(solution)/shard_map/pallas_call | solution.py:583
  83.0 1.5 %shard_map.87 = (f32[1,96,256]{2,1,0:T(8,128)}, f32[3,12]{1,0:T(4,128)}) custom-call(f32[1,96,256]{2,1,0:T(8,128)} %get-tuple-element.6.panel_in, f32[3,12]{1,0:T(4,128)} %get-tuple-element.7.hess_in), custom_call_target="tpu_custom_call" | custom-call | tf_op jit(solution)/shard_map/pallas_call | solution.py:609

commit v5 on v4

--- a/solution.py
+++ b/solution.py
@@ -500,6 +500,20 @@
         estimate_image = estimate_image + product(both_parts(estimate, pick(k)), nh[k], nl[k], NT)
     u = both_parts(estimate, p.col)
     estimate_full = estimate_image + product(u, nh[K], nl[K], NT)
+    def place_rows(at, values, images):
+        for j in range(PLANE):
+            padded[pl.ds(8 * j + at, 3)] = values[3 * j : 3 * j + 3]
+            padded_image[pl.ds(8 * j + at, 3)] = images[3 * j : 3 * j + 3]
+
+    for ref in (padded, padded_image):
+        ref[...] = jnp.zeros((8 * PLANE, B), F32)
+    fill = jnp.zeros((128 - C, B), F32)
+    for ref in (right, right_image):
+        ref[pl.ds(C, 128 - C)] = fill
+        ref[pl.ds(128 + C, 128 - C)] = fill
+    place_rows(0, u, estimate_image)
+    right[pl.ds(0, C)] = u
+    right_image[pl.ds(0, C)] = estimate_full
     for h in range(PARTS):
         gathers[2][h].end()
 
@@ -513,18 +527,10 @@
     direction_full = direction_image + product(d, nh[K], nl[K], NT)
     curve_next = stack_to_rows([side_sums([(d, 2.0 * half_image)])])
 
-    for j in range(PLANE):
-        rows3 = slice(3 * j, 3 * j + 3)
-        for ref, first_half, second_half in ((padded, u, d), (padded_image, estimate_image, direction_image)):
-            ref[pl.ds(8 * j, 3)] = first_half[rows3]
-            ref[pl.ds(8 * j + 3, 3)] = second_half[rows3]
-            ref[pl.ds(8 * j + 6, 2)] = jnp.zeros((2, B), F32)
-    fill = jnp.zeros((128 - C, B), F32)
-    right[...] = jnp.concatenate([u, fill, d, fill], axis=0)
-    right_image[...] = jnp.concatenate([estimate_full, fill, direction_full, fill], axis=0)
-    pair_sums = lax.dot_general(
-        padded[...], right_image[...], NT, precision=HIGHEST, preferred_element_type=F32
-    ) + lax.dot_general(padded_image[...], right[...], NT, precision=HIGHEST, preferred_element_type=F32)
+    place_rows(3, d, direction_image)
+    right[pl.ds(128, C)] = d
+    right_image[pl.ds(128, C)] = direction_full
+    pair_sums = product(padded[...], *split(right_image[...]), NT) + product(padded_image[...], *split(right[...]), NT)
     curve_row = jnp.concatenate([curve_next[0:1], jnp.zeros((1, 128), F32)], axis=1)
     row_of = lax.broadcasted_iota(I32, (8, 256), 0)
     for j in range(PLANE):

time: 84.7 us -> 84.6 us (level)
  no operation moved by 1% of the time
where the time goes in v5:
time: 84.6 us; the launch traced here: 84.5 us
  Pallas kernels  83.8 us (99%)
    pallas_call x1, Pallas kernels, on_device(): pl.pallas_call(kernel, out_shape=(jax.ShapeDtypeStruct((1, C, B), F32), j...  82.3 us

profile of v5, /device:TPU:1, one launch (start us, length us, event | category | flops | bytes accessed | tf_op | source)
XLA Modules:
  0.0 84.5 jit_solution(14659873176488918620)
XLA Ops:
  0.6 82.3 %shard_map.86 = (f32[1,96,256]{2,1,0:T(8,128)}, f32[3,12]{1,0:T(4,128)}) custom-call(f32[1,256,256]{2,1,0:T(8,128)} %diag_hbm.1, f32[1,7,256,256]{3,2,1,0:T(8,128)} %pairs_hbm.1, s32[1,7]{1,0:T(1,128)} %pattern.1, f32[1,256,256]{2,1,0:T(8,128)} %newton_diag_hbm.1, f32[1,7,256,256]{3,2,1,0:T(8,128)} %newton_pairs_hbm.1, f32[1,96,256]{2,1,0:T(8,128)} %warm_hbm.1, ...), custom_call_target="tpu_custom_call" | custom-call | tf_op jit(solution)/shard_map/pallas_call | solution.py:589
  82.9 1.5 %shard_map.87 = (f32[1,96,256]{2,1,0:T(8,128)}, f32[3,12]{1,0:T(4,128)}) custom-call(f32[1,96,256]{2,1,0:T(8,128)} %get-tuple-element.6.panel_in, f32[3,12]{1,0:T(4,128)} %get-tuple-element.7.hess_in), custom_call_target="tpu_custom_call" | custom-call | tf_op jit(solution)/shard_map/pallas_call | solution.py:615
